TPU v7x, 128 devices: a whole 4x4x4 slice. The times are simulated.
128 devices in a mesh: section: 2 (over core), lat: 8 (over z_lo, x), lon: 8 (over z_hi, y).
Axes of the slice: x: 4, y: 4, z: 4 (z_hi: 2, z_lo: 2; z = z_hi * 2 + z_lo), core: 2. Of those that a mesh axis runs over, the one named last changes fastest.
Arguments:
- level_tokens: bfloat16 [1, 8, 8, 8, 24, 13, 512], P(None, None, 'lat', None, 'lon'), may hold values from -6 to 6
- enc_query: bfloat16 [3, 512], replicated, may hold values from -6 to 6
- encoder_projection_weights: bfloat16 [4, 512, 512], replicated, may hold values from -0.25 to 0.25
- attn_proj: bfloat16 [2, 4, 512, 512], replicated, may hold values from -0.25 to 0.25
- expand_matrix_pair: bfloat16 [2, 512, 2048], replicated, may hold values from -0.25 to 0.25
- contract_matrix_pair: bfloat16 [2, 2048, 512], replicated, may hold values from -0.125 to 0.125
- normalization_gain_table: float32 [2, 2, 512], replicated, may hold values from 0.25 to 1.75
Outputs:
- predicted_latents: bfloat16 [1, 64, 192, 3, 512], P(None, 'lat', 'lon', None, 'section')
All inputs are finite; a program needn't handle non-finite values.
Results may differ from a plain program's by a relative error of at most 0.023.
Values may be sent and summed in bfloat16 or wider, within the bound.
No kernel may reach another device: no remote copies, remote signals or barrier semaphores. Data moves between devices by JAX's collectives and lax.ppermute only.
A program may use at most 128 MiB of HBM per device.

v0:
```python
import math

import jax
import jax.numpy as jnp
import numpy as np
from jax import lax
from jax.experimental import pallas as pl
from jax.experimental.pallas import tpu as pltpu
from jax.sharding import PartitionSpec as P

F32 = jnp.float32
BF16 = jnp.bfloat16
EPS = 1e-05
NEG = -1e30
HEADS = 16
HEAD = 32
GROUP = 8
LEVELS = 13
LATENTS = 3
D = 512
HALF = 256
FF = 2048
TOKENS = 144
QUAD = 36
CHUNK = 24
SCALE = math.log2(math.e) / math.sqrt(HEAD)
ALL_AXES = ("section", "lat", "lon")
VMEM_LIMIT = 56 * 1024 * 1024


def one_hot(rows, cols, pairs):
    out = np.zeros((rows, cols), np.float32)
    for row, col in pairs:
        out[row, col] = 1.0
    return out


def encoder_tables():
    cells = 24
    gather = one_hot(
        LEVELS * cells, 16 * cells,
        [(c * cells + i, i * 16 + c) for c in range(LEVELS) for i in range(cells)],
    )
    scatter = [
        one_hot(
            8 * CHUNK, LATENTS * cells,
            [
                (b * CHUNK + half * 9 + w * 3 + l, l * cells + b * 3 + w)
                for b in range(8) for w in range(3) for l in range(3)
            ],
        )
        for half in range(2)
    ]
    return gather, np.stack(scatter)


def compact_table():
    tables = []
    for half in range(2):
        pairs = []
        for rh in range(2):
            for ch in range(2):
                for r in range(2):
                    for c in range(6):
                        for l in range(3):
                            token = ((rh * 2 + ch) * 2 + r) * 18 + c * 3 + l
                            col = ch * 6 + c
                            chunk = (2 * rh + r) * 4 + col // 3
                            pairs.append((token, chunk * CHUNK + half * 9 + (col % 3) * 3 + l))
        tables.append(one_hot(TOKENS, 16 * CHUNK, pairs))
    return np.stack(tables)


def run(dst, src):
    return [(dst + i, src + i) for i in range(QUAD)]


def shifted_tables():
    source = np.stack([
        one_hot(144, 288, run(36, 0) + run(108, 144)),
        one_hot(144, 288, run(0, 36) + run(36, 72) + run(72, 180) + run(108, 216)),
        one_hot(144, 288, run(0, 108) + run(72, 252)),
    ])
    left = np.stack([
        one_hot(144, 144, run(0, 0) + run(72, 36)),
        one_hot(144, 144, run(0, 108) + run(72, 72)),
    ])
    right = np.stack([
        one_hot(144, 144, run(36, 0) + run(108, 36)),
        one_hot(144, 144, run(36, 108) + run(108, 72)),
    ])
    queries = one_hot(160, 144, run(0, 0) + run(40, 36) + run(76, 72) + run(112, 108))
    rowmajor = one_hot(
        144, 144,
        [
            (r * 72 + (cb * 6 + c) * 3 + l, cb * 36 + r * 18 + c * 3 + l)
            for cb in range(4) for r in range(2) for c in range(6) for l in range(3)
        ],
    )
    back = rowmajor @ queries.T
    return source, left, right, queries, back, rowmajor


def ones_table():
    out = np.zeros((1152, 256), np.float32)
    for h in range(GROUP):
        out[h * 128 : (h + 1) * 128, h * HEAD : (h + 1) * HEAD] = 1.0
        out[1024 + h * 16 : 1024 + (h + 1) * 16, h * HEAD : (h + 1) * HEAD] = 1.0
    return out


def dot(a, b):
    return jnp.dot(a, b, preferred_element_type=F32)


def pick(table, rows):
    return dot(table, rows).astype(BF16)


def normed(values, gain):
    center = values - jnp.mean(values, -1, keepdims=True)
    spread = jnp.mean(center * center, -1, keepdims=True)
    return (center * lax.rsqrt(spread + EPS) * gain).astype(BF16)


def gelu(x):
    return 0.5 * x * (1.0 + lax.erf(x * (1.0 / math.sqrt(2.0))))


def by_head(block):
    lane = lax.broadcasted_iota(jnp.int32, (1, HALF), 1) // HEAD
    main, rest = block[:128], block[128:]
    zero = jnp.zeros((), block.dtype)
    parts = [jnp.where(lane == h, main, zero) for h in range(GROUP)]
    parts += [jnp.where(lane == h, rest, zero) for h in range(GROUP)]
    return jnp.concatenate(parts, axis=0)


def attend(q, k, v, bias, ones):
    outs = []
    lane = lax.broadcasted_iota(jnp.int32, (1, 128), 1) // 16
    for g in range(HEADS // GROUP):
        cols = slice(g * HALF, (g + 1) * HALF)
        scores = lax.dot_general(
            q[:, cols], by_head(k[:, cols]), (((1,), (1,)), ((), ())),
            preferred_element_type=F32,
        )
        if bias is not None:
            scores = scores + bias
        tail = scores[:, 1024:]
        shift = jnp.zeros_like(tail)
        parts = []
        for h in range(GROUP):
            own = scores[:, h * 128 : (h + 1) * 128]
            top = jnp.max(
                jnp.maximum(own, jnp.where(lane == h, tail, -jnp.inf)), axis=-1, keepdims=True
            )
            parts.append(jnp.exp2(own - top).astype(BF16))
            shift = jnp.where(lane == h, top, shift)
        parts.append(jnp.exp2(tail - shift).astype(BF16))
        weights = jnp.concatenate(parts, axis=1)
        outs.append(dot(weights, by_head(v[:, cols])) / dot(weights, ones))
    return jnp.concatenate(outs, axis=1)


def feed_forward(tokens, w_in, w_out):
    total = None
    step = 512
    for i in range(FF // step):
        cols = slice(i * step, (i + 1) * step)
        hidden = gelu(dot(tokens, w_in[:, cols])).astype(BF16)
        part = dot(hidden, w_out[cols, :])
        total = part if total is None else total + part
    return total


def encode_kernel(x_ref, query_ref, w_ref, gather_ref, scatter_ref, out_ref, rows, weights):
    section = lax.axis_index("section")
    half = pl.ds(pl.multiple_of(section * HALF, HALF), HALF)

    @pl.when(pl.program_id(0) == 0)
    def _():
        rows[...] = jnp.zeros_like(rows)
        query = jnp.concatenate([query_ref[...], jnp.zeros((5, D), BF16)], axis=0)
        latent = dot(query, w_ref[0, :, half]).astype(BF16).astype(F32)
        turned = latent.T
        keys = w_ref[1, :, half]
        weights[:, :HALF] = w_ref[2, :, half]
        same = (
            lax.broadcasted_iota(jnp.int32, (HALF, HALF), 0) // HEAD
            == lax.broadcasted_iota(jnp.int32, (HALF, HALF), 1) // HEAD
        )
        for l in range(LATENTS):
            spread = jnp.where(same, turned[:, l : l + 1], 0.0).astype(BF16)
            weights[:, HALF * (l + 1) : HALF * (l + 2)] = (dot(keys, spread) * SCALE).astype(BF16)

    for i in range(24):
        rows[16 * i : 16 * i + LEVELS, :] = x_ref[i]
    tokens = pick(gather_ref[...], rows[...])
    mixed = []
    value = dot(tokens, weights[:, :HALF]).reshape(LEVELS, 24, HALF)
    for l in range(LATENTS):
        scores = dot(tokens, weights[:, HALF * (l + 1) : HALF * (l + 2)])
        scores = scores.reshape(LEVELS, 24, HALF)
        expd = jnp.exp2(scores - jnp.max(scores, axis=0, keepdims=True))
        mixed.append(jnp.sum(expd * value, axis=0) / jnp.sum(expd, axis=0))
    mixed = jnp.concatenate(mixed, axis=0).astype(BF16)
    out_ref[...] = (
        dot(scatter_ref[0], mixed[:, :128]) + dot(scatter_ref[1], mixed[:, 128:])
    ).astype(BF16)


def encode(level_tokens, enc_query, weights):
    cells = level_tokens.shape[1] * level_tokens.shape[3] * level_tokens.shape[4]
    source = level_tokens.reshape(cells, LEVELS, D)
    gather, scatter = encoder_tables()
    steps = cells // 24
    return pl.pallas_call(
        encode_kernel,
        grid=(steps,),
        out_shape=jax.ShapeDtypeStruct((steps * 8 * CHUNK, 128), BF16),
        in_specs=[
            pl.BlockSpec((24, LEVELS, D), lambda i: (i, 0, 0)),
            pl.BlockSpec((LATENTS, D), lambda i: (0, 0)),
            pl.BlockSpec((3, D, D), lambda i: (0, 0, 0)),
            pl.BlockSpec(gather.shape, lambda i: (0, 0)),
            pl.BlockSpec(scatter.shape, lambda i: (0, 0, 0)),
        ],
        out_specs=pl.BlockSpec((8 * CHUNK, 128), lambda i: (i, 0)),
        scratch_shapes=[pltpu.VMEM((24 * 16, D), BF16), pltpu.VMEM((D, 4 * HALF), BF16)],
        compiler_params=pltpu.CompilerParams(vmem_limit_bytes=VMEM_LIMIT),
        name="encode_levels",
    )(source, enc_query, weights, jnp.asarray(gather, BF16), jnp.asarray(scatter, BF16))


def first_kernel(
    own_ref, other_ref, query_ref, gain_ref, compact_ref, ones_ref,
    enc_hbm, proj_hbm, in_hbm, out_hbm, x_ref, enc_w, proj, w_in, w_out, sems,
):
    section = lax.axis_index("section")
    copies = [
        pltpu.make_async_copy(enc_hbm.at[3], enc_w, sems.at[0]),
        pltpu.make_async_copy(proj_hbm.at[0], proj, sems.at[1]),
        pltpu.make_async_copy(in_hbm.at[0], w_in, sems.at[2]),
        pltpu.make_async_copy(out_hbm.at[0], w_out, sems.at[3]),
    ]
    for copy in copies:
        copy.start()

    def gathered(ref):
        out = []
        for w in range(2):
            parts = []
            for r in range(4):
                start = pl.multiple_of((section * 4 + r) * 8 * CHUNK + w * 4 * CHUNK, 32)
                parts.append(ref[pl.ds(start, 4 * CHUNK), :])
            block = jnp.concatenate(parts, axis=0)
            out.append(
                jnp.concatenate(
                    [dot(compact_ref[0], block), dot(compact_ref[1], block)], axis=1
                ).astype(BF16)
            )
        return jnp.concatenate(out, axis=0)

    own, other = gathered(own_ref), gathered(other_ref)
    latent = lax.broadcasted_iota(jnp.int32, (2 * TOKENS, 1), 0) % LATENTS
    query = query_ref[...].astype(F32)
    base = jnp.where(
        latent == 0, query[0:1], jnp.where(latent == 1, query[1:2], query[2:3])
    )
    copies[0].wait()
    mine = pl.ds(pl.multiple_of(section * HALF, HALF), HALF)
    theirs = pl.ds(pl.multiple_of((1 - section) * HALF, HALF), HALF)
    tokens = base + dot(own, enc_w[mine, :]) + dot(other, enc_w[theirs, :])
    tokens = tokens.astype(BF16).astype(F32)
    flat = normed(tokens, gain_ref[0, 0:1, :])
    copies[1].wait()
    q = (dot(flat, proj[0]) * SCALE).astype(BF16)
    k = dot(flat, proj[1]).astype(BF16)
    v = dot(flat, proj[2]).astype(BF16)
    mixed = []
    for w in range(2):
        part = slice(w * TOKENS, (w + 1) * TOKENS)
        mixed.append(attend(q[part], k[part], v[part], None, ones_ref[...]))
    mixed = jnp.concatenate(mixed, axis=0).astype(BF16)
    middle = (tokens + dot(mixed, proj[3]).astype(BF16).astype(F32)).astype(BF16).astype(F32)
    flat = normed(middle, gain_ref[0, 1:2, :])
    copies[2].wait()
    copies[3].wait()
    done = middle + feed_forward(flat, w_in, w_out)
    done = jnp.concatenate([done[0:72], done[144:216], done[72:144], done[216:288]], axis=0)
    x_ref[...] = done.astype(BF16)


def vmem():
    return pl.BlockSpec(memory_space=pltpu.VMEM)


def hbm():
    return pl.BlockSpec(memory_space=pl.ANY)


def first_layer(own, other, enc_query, gains, enc_w, proj, w_in, w_out):
    return pl.pallas_call(
        first_kernel,
        out_shape=jax.ShapeDtypeStruct((2 * TOKENS, D), BF16),
        in_specs=[vmem()] * 6 + [hbm()] * 4,
        out_specs=vmem(),
        scratch_shapes=[
            pltpu.VMEM((D, D), BF16),
            pltpu.VMEM((4, D, D), BF16),
            pltpu.VMEM((D, FF), BF16),
            pltpu.VMEM((FF, D), BF16),
            pltpu.SemaphoreType.DMA((4,)),
        ],
        compiler_params=pltpu.CompilerParams(vmem_limit_bytes=VMEM_LIMIT),
        name="first_layer",
    )(
        own, other, enc_query, gains,
        jnp.asarray(compact_table(), BF16), jnp.asarray(ones_table(), BF16),
        enc_w, proj, w_in, w_out,
    )


def second_kernel(
    above_ref, x_ref, below_ref, left_ref, right_ref, gain_ref,
    source_ref, pleft_ref, pright_ref, queries_ref, back_ref, rowmajor_ref, ones_ref,
    proj_hbm, in_hbm, out_hbm, keep_ref, send_ref, proj, w_in, w_out, sems,
):
    section = lax.axis_index("section")
    lat = lax.axis_index("lat")
    copies = [
        pltpu.make_async_copy(proj_hbm.at[1], proj, sems.at[0]),
        pltpu.make_async_copy(in_hbm.at[1], w_in, sems.at[1]),
        pltpu.make_async_copy(out_hbm.at[1], w_out, sems.at[2]),
    ]
    for copy in copies:
        copy.start()
    gain = gain_ref[1, 0:1, :]
    outer = [normed(ref[...].astype(F32), gain) for ref in (above_ref, below_ref)]
    own = normed(x_ref[...].astype(F32), gain)
    own = [own[:TOKENS], own[TOKENS:]]
    left = normed(left_ref[...].astype(F32), gain)
    right = normed(right_ref[...].astype(F32), gain)
    keys, asks = [], []
    for r in range(2):
        block = jnp.concatenate([outer[r], own[r]], axis=0)
        keys.append((dot(source_ref[0], block) + dot(pleft_ref[r], left)).astype(BF16))
        keys.append(pick(source_ref[1], block))
        keys.append((dot(source_ref[2], block) + dot(pright_ref[r], right)).astype(BF16))
        asks.append(pick(queries_ref[...], own[r]))
    keys = jnp.concatenate(keys, axis=0)
    asks = jnp.concatenate(asks, axis=0)
    copies[0].wait()
    q = dot(asks, proj[0]) * SCALE
    k = dot(keys, proj[1]).astype(BF16)
    v = dot(keys, proj[2]).astype(BF16)
    lane = lax.broadcasted_iota(jnp.int32, (1, 1152), 1)
    outside = (lane < 1024) & (lane % 128 < TOKENS // 2)
    edge = [(lat == 0) & (section == 0), (lat == lax.axis_size("lat") - 1) & (section == 1)]
    mixed = []
    for r in range(2):
        bias = jnp.where(outside & edge[r], NEG, 0.0)
        parts = []
        for c, (start, size) in enumerate(((0, 40), (40, 72), (112, 40))):
            part = slice((3 * r + c) * TOKENS, (3 * r + c + 1) * TOKENS)
            asked = q[r * 160 + start : r * 160 + start + size].astype(BF16)
            parts.append(attend(asked, k[part], v[part], bias, ones_ref[...]))
        parts.append(jnp.zeros((8, D), F32))
        mixed.append(pick(back_ref[...], jnp.concatenate(parts, axis=0).astype(BF16)))
    mixed = jnp.concatenate(mixed, axis=0)
    before = jnp.concatenate(
        [dot(rowmajor_ref[...], x_ref[r * TOKENS : (r + 1) * TOKENS, :]) for r in range(2)], axis=0
    )
    middle = (before + dot(mixed, proj[3]).astype(BF16).astype(F32)).astype(BF16).astype(F32)
    flat = normed(middle, gain_ref[1, 1:2, :])
    copies[1].wait()
    copies[2].wait()
    done = (middle + feed_forward(flat, w_in, w_out)).astype(BF16)
    low, high = done[:, :HALF], done[:, HALF:]
    keep_ref[...] = jnp.where(section == 0, low, high)
    send_ref[...] = jnp.where(section == 0, high, low)


def second_layer(above, x, below, left, right, gains, proj, w_in, w_out):
    tables = [jnp.asarray(t, BF16) for t in shifted_tables() + (ones_table(),)]
    return pl.pallas_call(
        second_kernel,
        out_shape=[jax.ShapeDtypeStruct((2 * TOKENS, HALF), BF16)] * 2,
        in_specs=[vmem()] * 13 + [hbm()] * 3,
        out_specs=[vmem()] * 2,
        scratch_shapes=[
            pltpu.VMEM((4, D, D), BF16),
            pltpu.VMEM((D, FF), BF16),
            pltpu.VMEM((FF, D), BF16),
            pltpu.SemaphoreType.DMA((3,)),
        ],
        compiler_params=pltpu.CompilerParams(vmem_limit_bytes=VMEM_LIMIT),
        name="second_layer",
    )(above, x, below, left, right, gains, *tables, proj, w_in, w_out)


def swap(value):
    return lax.ppermute(value, "section", [(0, 1), (1, 0)])


def device_number(section, lat, lon):
    return (section * lax.axis_size("lat") + lat) * lax.axis_size("lon") + lon


def move_rows(value, step):
    lats, lons = lax.axis_size("lat"), lax.axis_size("lon")
    pairs = []
    for place in range(2 * lats):
        target = place + step
        if 0 <= target < 2 * lats:
            for lon in range(lons):
                pairs.append(
                    (
                        device_number(place % 2, place // 2, lon),
                        device_number(target % 2, target // 2, lon),
                    )
                )
    return lax.ppermute(value, ALL_AXES, pairs)


def move_cols(value, step):
    lons = lax.axis_size("lon")
    return lax.ppermute(value, "lon", [(i, (i + step) % lons) for i in range(lons)])


def on_device(
    level_tokens, enc_query, enc_weights, attn_proj, expand, contract, gains,
):
    section = lax.axis_index("section")
    pieces = encode(level_tokens, enc_query, enc_weights)
    own = lax.all_to_all(
        pieces.reshape(64, CHUNK, 128), ("lat", "lon"), split_axis=0, concat_axis=0, tiled=True
    )
    other = swap(own)
    rows = 64 * CHUNK
    x = first_layer(
        own.reshape(rows, 128), other.reshape(rows, 128), enc_query, gains,
        enc_weights, attn_proj, expand, contract,
    )
    below = move_rows(x[:TOKENS], -1)
    above = move_rows(x[TOKENS:], 1)
    bands = (above, x[:TOKENS], x[TOKENS:], below)
    right = move_cols(jnp.concatenate([band[:QUAD] for band in bands], axis=0), -1)
    left = move_cols(jnp.concatenate([band[3 * QUAD :] for band in bands], axis=0), 1)
    keep, send = second_layer(above, x, below, left, right, gains, attn_proj, expand, contract)
    got = swap(send)
    top = jnp.where(section == 0, keep, got)
    bottom = jnp.where(section == 0, got, keep)
    return jnp.concatenate([top, bottom], axis=0).reshape(1, 8, 24, LATENTS, HALF)


def solution(mesh):
    return jax.shard_map(
        on_device,
        mesh=mesh,
        in_specs=(P(None, None, "lat", None, "lon", None, None), P(), P(), P(), P(), P(), P()),
        out_specs=P(None, "lat", "lon", None, "section"),
        check_vma=False,
    )
```

profile of v0, /device:TPU:7, one launch (start us, length us, event | category | flops | bytes accessed | tf_op | source)
XLA Modules:
  0.0 92.8 jit_solution(10715217879048109577)
XLA Ops:
  0.0 4.4 %copy.21 = bf16[1,8,1,8,3,13,512]{6,5,4,3,1,2,0:T(8,128)(2,1)} copy(bf16[1,8,1,8,3,13,512]{6,3,5,4,2,1,0:T(8,128)(2,1)} %param.18) | data formatting | bytes 5111808 | tf_op args[0]
  4.4 11.5 %encode_levels.1 = bf16[1536,128]{1,0:T(8,128)(2,1)} custom-call(bf16[192,13,512]{2,1,0:T(8,128)(2,1)} %bitcast.4, bf16[3,512]{1,0:T(4,128)(2,1)} %query_ref.3, bf16[4,512,512]{2,1,0:T(8,128)(2,1)} %enc_hbm.1, bf16[312,384]{1,0:T(8,128)(2,1)} %constant.28.clone.gather_ref, bf16[2,192,72]{2,1,0:T(8,128)(2,1)} %constant.29.clone.scatter_ref), custom_call_target="tpu_custom_call" | custom-call | tf_op jit(solution)/shard_map/encode_levels/pallas_call | solution.py:218
  16.0 19.3 %all_to_all.5 = bf16[64,24,128]{2,1,0:T(8,128)(2,1)S(1)} all-to-all(bf16[64,24,128]{2,1,0:T(8,128)(2,1)} %bitcast.5), channel_id=1, replica_groups=mesh['section'=2,'lat'=8,'lon'=8] {'lat','lon'}, dimensions={0} | all-to-all | bytes 786432 | tf_op jit(solution)/shard_map/all_to_all | solution.py:437
  35.3 2.6 %collective-permute-start = (bf16[64,24,128]{2,1,0:T(8,128)(2,1)S(1)}, bf16[64,24,128]{2,1,0:T(8,128)(2,1)S(1)}, u32[]{:S(2)}, u32[]{:S(2)}) collective-permute-start(bf16[64,24,128]{2,1,0:T(8,128)(2,1)S(1)} %all_to_all.5), channel_id=1, source_target_pairs={{0,64},{64,0},{1,65},{65,1},{2,66},{66,2},{3,67},{67,3},{4,68},{68... | collective-permute-start | bytes 1179656 | tf_op jit(solution)/shard_map/ppermute | solution.py:404
  37.9 1.3 %collective-permute-done = bf16[64,24,128]{2,1,0:T(8,128)(2,1)S(1)} collective-permute-done((bf16[64,24,128]{2,1,0:T(8,128)(2,1)S(1)}, bf16[64,24,128]{2,1,0:T(8,128)(2,1)S(1)}, u32[]{:S(2)}, u32[]{:S(2)}) %collective-permute-start) | collective-permute-done | bytes 393248 | tf_op jit(solution)/shard_map/ppermute | solution.py:404
  39.3 0.7 copy-done.1
  40.0 9.0 %first_layer.1.x_ref = bf16[288,512]{1,0:T(8,128)(2,1)} custom-call(bf16[1536,128]{1,0:T(8,128)(2,1)} %bitcast.6, bf16[1536,128]{1,0:T(8,128)(2,1)} %bitcast.7, bf16[3,512]{1,0:T(4,128)(2,1)} %query_ref.3, f32[2,2,512]{2,1,0:T(2,128)} %gain_ref.3, bf16[2,144,384]{2,1,0:T(8,128)(2,1)} %constant.30.clone.compact_ref, ...), custom_call_target="tpu_custom_call" | custom-call | tf_op jit(solution)/shard_map/first_layer/pallas_call | solution.py:304
  49.0 1.0 %fusion.1 = (bf16[144,512]{1,0:T(8,128)(2,1)S(1)}, bf16[144,512]{1,0:T(8,128)(2,1)S(1)}) fusion(bf16[288,512]{1,0:T(8,128)(2,1)} %first_layer.1.x_ref), kind=kLoop, calls=%fused_computation.6 | loop fusion | bytes 589824 | tf_op jit(solution)/shard_map/slice | solution.py:446
  50.0 4.5 %collective-permute-start.1 = (bf16[144,512]{1,0:T(8,128)(2,1)S(1)}, bf16[144,512]{1,0:T(8,128)(2,1)S(1)}, u32[]{:S(2)}, u32[]{:S(2)}) collective-permute-start(bf16[144,512]{1,0:T(8,128)(2,1)S(1)} %get-tuple-element.16), channel_id=1, source_target_pairs={{0,64},{1,65},{2,66},{3,67},{4,68},{5,69},{6,70},{7,71},{64,8},{65... | collective-permute-start | bytes 442376 | tf_op jit(solution)/shard_map/ppermute | solution.py:424
  54.5 1.9 %collective-permute-start.2 = (bf16[144,512]{1,0:T(8,128)(2,1)S(1)}, bf16[144,512]{1,0:T(8,128)(2,1)S(1)}, u32[]{:S(2)}, u32[]{:S(2)}) collective-permute-start(bf16[144,512]{1,0:T(8,128)(2,1)S(1)} %get-tuple-element.15), channel_id=1, source_target_pairs={{64,0},{65,1},{66,2},{67,3},{68,4},{69,5},{70,6},{71,7},{8,64},{9,... | collective-permute-start | bytes 442376 | tf_op jit(solution)/shard_map/ppermute | solution.py:424
  56.4 0.9 fusion
  57.3 0.0 collective-permute-done.1.above_ref
  57.4 5.9 %collective-permute-done.2.below_ref = bf16[144,512]{1,0:T(8,128)(2,1)S(1)} collective-permute-done((bf16[144,512]{1,0:T(8,128)(2,1)S(1)}, bf16[144,512]{1,0:T(8,128)(2,1)S(1)}, u32[]{:S(2)}, u32[]{:S(2)}) %collective-permute-start.2) | collective-permute-done | bytes 147488 | tf_op jit(solution)/shard_map/ppermute | solution.py:424
  63.4 3.1 %collective-permute-start.4 = (bf16[144,512]{1,0:T(8,128)(2,1)S(1)}, bf16[144,512]{1,0:T(8,128)(2,1)S(1)}, u32[]{:S(2)}, u32[]{:S(2)}) collective-permute-start(bf16[144,512]{1,0:T(8,128)(2,1)S(1)} %pad_maximum_fusion.2), channel_id=1, source_target_pairs={{0,7},{1,0},{2,1},{3,2},{4,3},{5,4},{6,5},{7,6},{8,15},{9,8},{10,9... | collective-permute-start | bytes 442376 | tf_op jit(solution)/shard_map/ppermute | solution.py:429
  66.5 0.3 collective-permute-start.3
  66.8 1.8 %collective-permute-done.4.right_ref = bf16[144,512]{1,0:T(8,128)(2,1)S(1)} collective-permute-done((bf16[144,512]{1,0:T(8,128)(2,1)S(1)}, bf16[144,512]{1,0:T(8,128)(2,1)S(1)}, u32[]{:S(2)}, u32[]{:S(2)}) %collective-permute-start.4) | collective-permute-done | bytes 147488 | tf_op jit(solution)/shard_map/ppermute | solution.py:429
  68.6 5.8 %collective-permute-done.3.left_ref = bf16[144,512]{1,0:T(8,128)(2,1)S(1)} collective-permute-done((bf16[144,512]{1,0:T(8,128)(2,1)S(1)}, bf16[144,512]{1,0:T(8,128)(2,1)S(1)}, u32[]{:S(2)}, u32[]{:S(2)}) %collective-permute-start.3) | collective-permute-done | bytes 147488 | tf_op jit(solution)/shard_map/ppermute | solution.py:429
  74.4 0.6 copy-done.5
  75.0 14.2 %second_layer.1 = (bf16[288,256]{1,0:T(8,128)(2,1)}, bf16[288,256]{1,0:T(8,128)(2,1)}) custom-call(bf16[144,512]{1,0:T(8,128)(2,1)} %copy-done.2, bf16[288,512]{1,0:T(8,128)(2,1)} %first_layer.1.x_ref, bf16[144,512]{1,0:T(8,128)(2,1)} %copy-done.3, bf16[144,512]{1,0:T(8,128)(2,1)} %copy-done.5, bf16[144,512]{1,0:T(8,128)(2,1)} %copy-done.4, ...), custom_call_target="tpu_custom_call" | custom-call | tf_op jit(solution)/shard_map/second_layer/pallas_call | solution.py:387
  89.3 0.1 collective-permute-start.5
  89.3 1.6 %collective-permute-done.5 = bf16[288,256]{1,0:T(8,128)(2,1)S(1)} collective-permute-done((bf16[288,256]{1,0:T(8,128)(2,1)}, bf16[288,256]{1,0:T(8,128)(2,1)S(1)}, u32[]{:S(2)}, u32[]{:S(2)}) %collective-permute-start.5) | collective-permute-done | bytes 147488 | tf_op jit(solution)/shard_map/ppermute | solution.py:404
  90.9 0.9 %broadcast_select_fusion.1 = (bf16[288,256]{1,0:T(8,128)(2,1)S(1)}, bf16[288,256]{1,0:T(8,128)(2,1)S(1)}) fusion(bf16[288,256]{1,0:T(8,128)(2,1)} %get-tuple-element.7, bf16[288,256]{1,0:T(8,128)(2,1)S(1)} %collective-permute-done.5, pred[]{:T(512)S(6)} %eq.4), kind=kLoop, calls=%fused_computation.4 | loop fusion | flops 147456 | bytes 589825 | tf_op jit(solution)/shard_map/jit(_where)/select_n | solution.py:453
  91.9 0.1 reshape.19
  92.0 0.8 copy.22
  (15 shorter events, 0.1 us)
Async XLA Ops:
  35.3 4.0 %copy-start = (bf16[64,24,128]{2,1,0:T(8,128)(2,1)}, bf16[64,24,128]{2,1,0:T(8,128)(2,1)S(1)}, u32[]{:S(2)}) copy-start(bf16[64,24,128]{2,1,0:T(8,128)(2,1)S(1)} %all_to_all.5) | copy-start | bytes 1179652
  35.3 4.0 %collective-permute-start = (bf16[64,24,128]{2,1,0:T(8,128)(2,1)S(1)}, bf16[64,24,128]{2,1,0:T(8,128)(2,1)S(1)}, u32[]{:S(2)}, u32[]{:S(2)}) collective-permute-start(bf16[64,24,128]{2,1,0:T(8,128)(2,1)S(1)} %all_to_all.5), channel_id=1, source_target_pairs={{0,64},{64,0},{1,65},{65,1},{2,66},{66,2},{3,67},{67,3},{4,68},{68... | collective-permute-start | bytes 1179656 | tf_op jit(solution)/shard_map/ppermute | solution.py:404
  39.3 0.7 copy-start.1
  50.0 7.4 %collective-permute-start.1 = (bf16[144,512]{1,0:T(8,128)(2,1)S(1)}, bf16[144,512]{1,0:T(8,128)(2,1)S(1)}, u32[]{:S(2)}, u32[]{:S(2)}) collective-permute-start(bf16[144,512]{1,0:T(8,128)(2,1)S(1)} %get-tuple-element.16), channel_id=1, source_target_pairs={{0,64},{1,65},{2,66},{3,67},{4,68},{5,69},{6,70},{7,71},{64,8},{65... | collective-permute-start | bytes 442376 | tf_op jit(solution)/shard_map/ppermute | solution.py:424
  54.5 8.8 %collective-permute-start.2 = (bf16[144,512]{1,0:T(8,128)(2,1)S(1)}, bf16[144,512]{1,0:T(8,128)(2,1)S(1)}, u32[]{:S(2)}, u32[]{:S(2)}) collective-permute-start(bf16[144,512]{1,0:T(8,128)(2,1)S(1)} %get-tuple-element.15), channel_id=1, source_target_pairs={{64,0},{65,1},{66,2},{67,3},{68,4},{69,5},{70,6},{71,7},{8,64},{9,... | collective-permute-start | bytes 442376 | tf_op jit(solution)/shard_map/ppermute | solution.py:424
  57.4 17.0 %copy-start.2 = (bf16[144,512]{1,0:T(8,128)(2,1)}, bf16[144,512]{1,0:T(8,128)(2,1)S(1)}, u32[]{:S(2)}) copy-start(bf16[144,512]{1,0:T(8,128)(2,1)S(1)} %collective-permute-done.1.above_ref) | copy-start | bytes 442372
  63.3 11.1 %copy-start.3 = (bf16[144,512]{1,0:T(8,128)(2,1)}, bf16[144,512]{1,0:T(8,128)(2,1)S(1)}, u32[]{:S(2)}) copy-start(bf16[144,512]{1,0:T(8,128)(2,1)S(1)} %collective-permute-done.2.below_ref) | copy-start | bytes 442372
  63.4 5.2 %collective-permute-start.4 = (bf16[144,512]{1,0:T(8,128)(2,1)S(1)}, bf16[144,512]{1,0:T(8,128)(2,1)S(1)}, u32[]{:S(2)}, u32[]{:S(2)}) collective-permute-start(bf16[144,512]{1,0:T(8,128)(2,1)S(1)} %pad_maximum_fusion.2), channel_id=1, source_target_pairs={{0,7},{1,0},{2,1},{3,2},{4,3},{5,4},{6,5},{7,6},{8,15},{9,8},{10,9... | collective-permute-start | bytes 442376 | tf_op jit(solution)/shard_map/ppermute | solution.py:429
  66.5 7.9 %collective-permute-start.3 = (bf16[144,512]{1,0:T(8,128)(2,1)S(1)}, bf16[144,512]{1,0:T(8,128)(2,1)S(1)}, u32[]{:S(2)}, u32[]{:S(2)}) collective-permute-start(bf16[144,512]{1,0:T(8,128)(2,1)S(1)} %pad_maximum_fusion.1), channel_id=1, source_target_pairs={{0,1},{1,2},{2,3},{3,4},{4,5},{5,6},{6,7},{7,0},{8,9},{9,10},{10,1... | collective-permute-start | bytes 442376 | tf_op jit(solution)/shard_map/ppermute | solution.py:429
  68.6 5.8 %copy-start.4 = (bf16[144,512]{1,0:T(8,128)(2,1)}, bf16[144,512]{1,0:T(8,128)(2,1)S(1)}, u32[]{:S(2)}) copy-start(bf16[144,512]{1,0:T(8,128)(2,1)S(1)} %collective-permute-done.4.right_ref) | copy-start | bytes 442372
  74.4 0.7 copy-start.5
  89.3 1.7 %collective-permute-start.5 = (bf16[288,256]{1,0:T(8,128)(2,1)}, bf16[288,256]{1,0:T(8,128)(2,1)S(1)}, u32[]{:S(2)}, u32[]{:S(2)}) collective-permute-start(bf16[288,256]{1,0:T(8,128)(2,1)} %get-tuple-element.8), channel_id=1, source_target_pairs={{0,64},{64,0},{1,65},{65,1},{2,66},{66,2},{3,67},{67,3},{4,68},{68... | collective-permute-start | bytes 442376 | tf_op jit(solution)/shard_map/ppermute | solution.py:404
where the time goes:
time: 93.3 us; the launch traced here: 92.8 us
  Pallas kernels  34.7 us (37%)
  blocking collectives  19.3 us (21%)
  waiting for transfers between devices  16.4 us (18%)
  starting transfers between devices  12.5 us (13%)
  local copies, waits for them, and re-layouts  8.68 us (9%)
  other arithmetic  1.02 us (1%)
    all_to_all x1, blocking collectives, on_device(): lax.all_to_all(pieces.reshape(64, CHUNK, 128), ('lat', 'lon'), split_axis...  19.3 us
    pallas_call x1, Pallas kernels, second_layer(): pl.pallas_call(second_kernel, out_shape=[jax.ShapeDtypeStruct((2 * TOKENS...  14.2 us
    pallas_call x1, Pallas kernels, encode(): pl.pallas_call(encode_kernel, grid=(steps,), out_shape=jax.ShapeDtypeStru...  11.5 us
    pallas_call x1, Pallas kernels, first_layer(): pl.pallas_call(first_kernel, out_shape=jax.ShapeDtypeStruct((2 * TOKENS,...  8.98 us
    ppermute x2, waiting for transfers between devices, move_cols(): lax.ppermute(value, 'lon', [(i, (i + step) % lons) for i in range(lons)])  7.59 us
    ppermute x2, starting transfers between devices, move_rows(): return lax.ppermute(value, ALL_AXES, pairs)  6.42 us
    ppermute x2, waiting for transfers between devices, move_rows(): return lax.ppermute(value, ALL_AXES, pairs)  5.92 us
    unnamed x13, local copies, waits for them, and re-layouts  5.85 us
  transfers between devices with their start and end apart: 6, of which 5 were waited for; matrix products, arithmetic and copies ran while one was open for 1% of the time, Pallas kernels for 0%

commit v1 on v0

v1 whole, which is shorter than its diff:
```python
import functools
import math

import jax
import jax.numpy as jnp
import numpy as np
from jax import lax
from jax.experimental import pallas as pl
from jax.experimental.pallas import tpu as pltpu
from jax.sharding import PartitionSpec as P

F32 = jnp.float32
BF16 = jnp.bfloat16
EPS = 1e-05
NEG = -1e30
HEADS = 16
HEAD = 32
GROUP = 8
LEVELS = 13
LATENTS = 3
D = 512
HALF = 256
FF = 2048
TOKENS = 144
CHUNK = 40
WIDE = 216
SCALE = math.log2(math.e) / math.sqrt(HEAD)
ALL_AXES = ("section", "lat", "lon")
VMEM_LIMIT = 24 * 1024 * 1024


def one_hot(rows, cols, pairs):
    out = np.zeros((rows, cols), np.float32)
    for row, col in pairs:
        out[row, col] = 1.0
    return out


def encoder_tables():
    expand = one_hot(
        128, LATENTS * HALF,
        [
            (l * GROUP + h, l * HALF + h * HEAD + e)
            for l in range(LATENTS) for h in range(GROUP) for e in range(HEAD)
        ],
    )
    scatter = [
        one_hot(
            8 * CHUNK, 72,
            [
                (b * CHUNK + half * 18 + d * 9 + w * 3 + l, l * 24 + w * 8 + (b + d * side) % 8)
                for b in range(8) for d in range(2) for w in range(3) for l in range(3)
            ],
        )
        for side in (1, -1) for half in range(2)
    ]
    return expand, np.stack(scatter)


def compact_table():
    tables = []
    for half in range(2):
        pairs = []
        for d in range(2):
            for r in range(4):
                for c in range(12):
                    for l in range(3):
                        token = ((c // 6) * 4 + r) * 18 + (c % 6) * 3 + l
                        row = half * 18 + d * 9 + (c % 3) * 3 + l
                        pairs.append((d * TOKENS + token, (r * 4 + c // 3) * CHUNK + row))
        tables.append(one_hot(2 * TOKENS, 16 * CHUNK, pairs))
    return np.stack(tables)


def band_tables():
    return np.stack([
        one_hot(WIDE, 2 * WIDE, [(cb * 36 + i, cb * 72 + rh * 36 + i) for cb in range(6) for i in range(36)])
        for rh in range(2)
    ])


def order_table():
    return one_hot(
        144, 160,
        [
            (r * 72 + l * 24 + cb * 6 + c, 4 + cb * 36 + r * 18 + c * 3 + l)
            for cb in range(4) for r in range(2) for c in range(6) for l in range(3)
        ],
    )


def dot(a, b):
    return jnp.dot(a, b, preferred_element_type=F32)


def pick(table, rows):
    return dot(table, rows).astype(BF16)


def normed_wide(values, gain):
    center = values - jnp.mean(values, -1, keepdims=True)
    spread = jnp.mean(center * center, -1, keepdims=True)
    return center * lax.rsqrt(spread + EPS) * gain


def normed(values, gain):
    return normed_wide(values, gain).astype(BF16)


def gelu(x):
    return 0.5 * x * (1.0 + lax.erf(x * (1.0 / math.sqrt(2.0))))


def by_head(block, heads=GROUP):
    lane = lax.broadcasted_iota(jnp.int32, (1, HALF), 1) // HEAD
    zero = jnp.zeros((), block.dtype)
    return jnp.concatenate([jnp.where(lane == h, block, zero) for h in range(heads)], axis=0)


def product_t(a, b):
    return lax.dot_general(a, b, (((1,), (1,)), ((), ())), preferred_element_type=F32)


def merge_heads(stack, count):
    lane = lax.broadcasted_iota(jnp.int32, (1, HALF), 1) // HEAD
    out = stack[:count]
    for h in range(1, GROUP):
        out = jnp.where(lane == h, stack[h * count : (h + 1) * count], out)
    return out


def attention_scores(q, k):
    return product_t(by_head(q).astype(BF16), k[:128]), product_t(q.astype(BF16), by_head(k[128:]))


def attention_weights(main, tail, bias):
    count = tail.shape[0]
    lane = lax.broadcasted_iota(jnp.int32, (1, 128), 1) // 16
    wide = lax.broadcasted_iota(jnp.int32, (1, HALF), 1) // HEAD
    if bias is not None:
        main = main + bias
    shift = jnp.zeros_like(tail)
    parts = []
    for h in range(GROUP):
        own = main[h * count : (h + 1) * count]
        top = jnp.max(
            jnp.maximum(own, jnp.where(lane == h, tail, -jnp.inf)), axis=-1, keepdims=True
        )
        parts.append(jnp.exp2(own - top))
        shift = jnp.where(lane == h, top, shift)
    rest = jnp.exp2(tail - shift)
    scale = jnp.zeros((count, HALF), F32)
    for h in range(GROUP):
        total = jnp.sum(parts[h] + jnp.where(lane == h, rest, 0.0), axis=-1, keepdims=True)
        scale = jnp.where(wide == h, total, scale)
    return jnp.concatenate(parts, axis=0).astype(BF16), rest.astype(BF16), scale


def attention_values(weights, rest, scale, v):
    total = merge_heads(dot(weights, v[:128]), scale.shape[0]) + dot(rest, by_head(v[128:]))
    return total / scale


def attend(windows, bias):
    groups = [slice(g * HALF, (g + 1) * HALF) for g in range(HEADS // GROUP)]
    jobs = [(q[:, g], k[:, g], v[:, g]) for q, k, v in windows for g in groups]
    scores, weights, outs = {}, {}, []
    for step in range(len(jobs) + 2):
        if step < len(jobs):
            scores[step] = attention_scores(*jobs[step][:2])
        if 1 <= step <= len(jobs):
            weights[step - 1] = attention_weights(*scores.pop(step - 1), bias)
        if step >= 2:
            outs.append(attention_values(*weights.pop(step - 2), jobs[step - 2][2]))
    return [
        jnp.concatenate(outs[i : i + len(groups)], axis=1)
        for i in range(0, len(outs), len(groups))
    ]


def windows_of(q, k, v, bounds):
    parts = [slice(w * TOKENS, (w + 1) * TOKENS) for w in range(len(bounds))]
    return [(q[a:b], k[part], v[part]) for (a, b), part in zip(bounds, parts)]


def feed_forward(tokens, w_in, w_out):
    total = None
    step = 512
    for i in range(FF // step):
        cols = slice(i * step, (i + 1) * step)
        hidden = gelu(dot(tokens, w_in[:, cols])).astype(BF16)
        part = dot(hidden, w_out[cols, :])
        total = part if total is None else total + part
    return total


def fetch(sources, targets, sems):
    return [
        pltpu.make_async_copy(source, target, sems.at[i])
        for i, (source, target) in enumerate(zip(sources, targets))
    ]


def encode_kernel(
    x_ref, query_ref, w_ref, expand_ref, scatter_ref, enc_hbm, in_hbm, out_hbm,
    out_ref, enc_next, in_next, out_next, keys, sems,
):
    side = lax.axis_index("lon") // 4
    copies = fetch(
        (enc_hbm.at[3], in_hbm.at[0], out_hbm.at[0]), (enc_next, in_next, out_next), sems
    )

    @pl.when(pl.program_id(0) == pl.num_programs(0) - 2)
    def _():
        for copy in copies:
            copy.start()

    @pl.when(pl.program_id(0) == 0)
    def _():
        query = jnp.concatenate([query_ref[...], jnp.zeros((5, D), BF16)], axis=0)
        latent = dot(query, w_ref[0]).astype(BF16).astype(F32)
        turned = latent.T
        col = lax.broadcasted_iota(jnp.int32, (HALF, 128), 1)
        head = lax.broadcasted_iota(jnp.int32, (HALF, 128), 0) // HEAD
        spread = jnp.zeros((HALF, 128), F32)
        for l in range(LATENTS):
            spread = jnp.where(col == l * GROUP + head, turned[:, l : l + 1], spread)
        keys[...] = (dot(w_ref[1], spread.astype(BF16)) * SCALE).astype(BF16)

    x = x_ref[...]
    rows = x.shape[0]
    count = rows // (LEVELS * 24)
    value = dot(x, w_ref[2])
    scores = dot(x, keys[...]).reshape(count * 3, LEVELS, 8, 128)
    expd = jnp.exp2(scores - jnp.max(scores, axis=1, keepdims=True))
    share = (expd / jnp.sum(expd, axis=1, keepdims=True)).reshape(rows, 128).astype(BF16)
    mixed = []
    for l in range(LATENTS):
        weighted = dot(share, expand_ref[:, l * HALF : (l + 1) * HALF]) * value
        mixed.append(jnp.sum(weighted.reshape(count * 3, LEVELS, 8, HALF), axis=1))
    for a in range(count):
        part = [m[3 * a : 3 * a + 3].reshape(24, HALF) for m in mixed]
        part = jnp.concatenate(part, axis=0).astype(BF16)
        out_ref[a * 8 * CHUNK : (a + 1) * 8 * CHUNK, :] = (
            dot(scatter_ref[2 * side], part[:, :128])
            + dot(scatter_ref[2 * side + 1], part[:, 128:])
        ).astype(BF16)

    @pl.when(pl.program_id(0) == pl.num_programs(0) - 1)
    def _():
        for copy in copies:
            copy.wait()


def vmem():
    return pl.BlockSpec(memory_space=pltpu.VMEM)


def hbm():
    return pl.BlockSpec(memory_space=pl.ANY)


def in_hbm_space(*arrays):
    return [pltpu.with_memory_space_constraint(a, pltpu.HBM) for a in arrays]


def encode(level_tokens, enc_query, enc_weights, expand, contract):
    source = level_tokens.transpose(0, 1, 2, 4, 5, 3, 6).reshape(-1, D)
    spread, scatter = encoder_tables()
    block = 2 * 24 * LEVELS
    steps = source.shape[0] // block
    return pl.pallas_call(
        encode_kernel,
        grid=(steps,),
        out_shape=[
            jax.ShapeDtypeStruct((steps * 16 * CHUNK, 128), BF16),
            pltpu.VMEM((D, D), BF16),
            pltpu.VMEM((D, FF), BF16),
            pltpu.VMEM((FF, D), BF16),
        ],
        in_specs=[
            pl.BlockSpec((block, D), lambda i: (i, 0)),
            pl.BlockSpec((LATENTS, D), lambda i: (0, 0)),
            pl.BlockSpec((3, D, HALF), lambda i: (0, 0, lax.axis_index("section"))),
            pl.BlockSpec(spread.shape, lambda i: (0, 0)),
            pl.BlockSpec(scatter.shape, lambda i: (0, 0, 0)),
        ] + [hbm()] * 3,
        out_specs=[pl.BlockSpec((16 * CHUNK, 128), lambda i: (i, 0))] + [hbm()] * 3,
        scratch_shapes=[pltpu.VMEM((D, 128), BF16), pltpu.SemaphoreType.DMA((3,))],
        compiler_params=pltpu.CompilerParams(vmem_limit_bytes=VMEM_LIMIT),
        name="encode_levels",
    )(
        *in_hbm_space(
            source, enc_query, enc_weights, jnp.asarray(spread, BF16), jnp.asarray(scatter, BF16),
            enc_weights, expand, contract,
        )
    )


def first_kernel(
    own_ref, other_ref, query_ref, gain_ref, compact_ref, bands_ref,
    proj_ref, enc_w, w_in, w_out, edge_ref, side_ref,
):
    proj = proj_ref.at[0]
    section = lax.axis_index("section")
    windows = []
    for group in range(2):
        parts = []
        for r in range(4):
            start = pl.multiple_of(((section * 4 + r) * 8 + group * 4) * CHUNK, 32)
            rows = pl.ds(start, 4 * CHUNK)
            parts.append(jnp.concatenate([own_ref[rows, :], other_ref[rows, :]], axis=1))
        block = jnp.concatenate(parts, axis=0)
        low, high = pick(compact_ref[0], block), pick(compact_ref[1], block)
        own = jnp.concatenate([low[:, :128], high[:, :128]], axis=1)
        other = jnp.concatenate([low[:, 128:], high[:, 128:]], axis=1)
        windows.append((own, other))
    own, other = [
        jnp.concatenate(
            [windows[1][i][TOKENS:], windows[0][i][:TOKENS], windows[1][i][:TOKENS], windows[0][i][TOKENS:]],
            axis=0,
        )
        for i in range(2)
    ]
    latent = lax.broadcasted_iota(jnp.int32, (4 * TOKENS, 1), 0) % LATENTS
    query = query_ref[...].astype(F32)
    base = jnp.where(
        latent == 0, query[0:1], jnp.where(latent == 1, query[1:2], query[2:3])
    )
    mine = pl.ds(pl.multiple_of(section * HALF, HALF), HALF)
    theirs = pl.ds(pl.multiple_of((1 - section) * HALF, HALF), HALF)
    tokens = base + dot(own, enc_w[mine, :]) + dot(other, enc_w[theirs, :])
    tokens = tokens.astype(BF16).astype(F32)
    wide = normed_wide(tokens, gain_ref[0, 0:1, :])
    flat = wide.astype(BF16)
    inner = slice(TOKENS // 2, 4 * TOKENS - TOKENS // 2)
    k = dot(flat, proj[1]).astype(BF16)
    v = dot(flat, proj[2]).astype(BF16)
    q = dot(wide[inner].astype(BF16), proj[0]) * SCALE
    bounds = ((0, 72), (72, 216), (216, 360), (360, 432))
    mixed = attend(windows_of(q, k, v, bounds), None)
    mixed = jnp.concatenate(mixed, axis=0).astype(BF16)
    middle = (tokens[inner] + dot(mixed, proj[3]).astype(BF16).astype(F32)).astype(BF16).astype(F32)
    flat = normed(middle, gain_ref[0, 1:2, :])
    done = (middle + feed_forward(flat, w_in, w_out)).astype(BF16)
    north, south = pick(bands_ref[0], done), pick(bands_ref[1], done)
    edge_ref[...] = jnp.where(section == 0, north, south)
    side_ref[...] = jnp.where(section == 0, south, north)


def first_layer(own, other, enc_query, gains, proj, weights):
    tables = [jnp.asarray(t, BF16) for t in (compact_table(), band_tables())]
    return pl.pallas_call(
        first_kernel,
        out_shape=[jax.ShapeDtypeStruct((WIDE, D), BF16)] * 2,
        in_specs=[vmem()] * 10,
        out_specs=[vmem()] * 2,
        compiler_params=pltpu.CompilerParams(vmem_limit_bytes=VMEM_LIMIT),
        name="first_layer",
    )(own, other, enc_query, gains, *tables, proj, *weights)


def side_kernel(
    halo_ref, own_ref, gain_ref, order_ref, proj_ref, in_hbm, out_hbm,
    keep_ref, send_ref, w_in, w_out, sems,
):
    copies = fetch((in_hbm.at[1], out_hbm.at[1]), (w_in, w_out), sems)
    second(
        False, copies, halo_ref, own_ref, gain_ref, order_ref, proj_ref.at[1], w_in, w_out,
        keep_ref, send_ref,
    )


def edge_kernel(
    halo_ref, own_ref, gain_ref, order_ref, proj_hbm, in_hbm, out_hbm,
    keep_ref, send_ref, w_in, w_out, proj, sems,
):
    copies = fetch(
        [proj_hbm.at[1, i] for i in (1, 2, 0, 3)] + [in_hbm.at[1], out_hbm.at[1]],
        [proj.at[i] for i in (1, 2, 0, 3)] + [w_in, w_out],
        sems,
    )
    second(
        True, copies, halo_ref, own_ref, gain_ref, order_ref, proj, w_in, w_out,
        keep_ref, send_ref,
    )


def second(
    at_edge, copies, halo_ref, own_ref, gain_ref, order_ref, proj, w_in, w_out,
    keep_ref, send_ref,
):
    for copy in copies:
        copy.start()
    section = lax.axis_index("section")
    gain = gain_ref[1, 0:1, :]
    halo = normed_wide(halo_ref[...].astype(F32), gain)
    own = normed_wide(own_ref[...].astype(F32), gain)
    keys = []
    for c in range(3):
        part = slice(72 * c, 72 * (c + 1))
        keys += [halo[part], own[part]]
    keys = jnp.concatenate(keys, axis=0).astype(BF16)
    for copy in copies[:-2]:
        copy.wait()
    q = dot(own[32:192].astype(BF16), proj[0]) * SCALE
    k = dot(keys, proj[1]).astype(BF16)
    v = dot(keys, proj[2]).astype(BF16)
    bias = None
    if at_edge:
        lat, last = lax.axis_index("lat"), lax.axis_size("lat") - 1
        pole = ((lat == 0) & (section == 0)) | ((lat == last) & (section == 1))
        outside = lax.broadcasted_iota(jnp.int32, (1, 128), 1) < TOKENS // 2
        bias = jnp.where(outside & pole, NEG, 0.0)
    mixed = attend(windows_of(q, k, v, ((0, 40), (40, 112), (112, 152))), bias)
    mixed.append(jnp.zeros((8, D), F32))
    mixed = pick(order_ref[...], jnp.concatenate(mixed, axis=0).astype(BF16))
    before = dot(order_ref[...], own_ref[32:192, :])
    middle = (before + dot(mixed, proj[3]).astype(BF16).astype(F32)).astype(BF16).astype(F32)
    flat = normed(middle, gain_ref[1, 1:2, :])
    for copy in copies[-2:]:
        copy.wait()
    done = (middle + feed_forward(flat, w_in, w_out)).astype(BF16)
    low, high = done[:, :HALF], done[:, HALF:]
    keep_ref[...] = jnp.where(section == 0, low, high)
    send_ref[...] = jnp.where(section == 0, high, low)


def second_layer(at_edge, halo, own, gains, order, proj, expand, contract):
    far = in_hbm_space(expand, contract)
    scratch = [pltpu.VMEM((D, FF), BF16), pltpu.VMEM((FF, D), BF16)]
    if at_edge:
        (proj,) = in_hbm_space(proj)
        scratch.append(pltpu.VMEM((4, D, D), BF16))
    return pl.pallas_call(
        edge_kernel if at_edge else side_kernel,
        out_shape=[jax.ShapeDtypeStruct((TOKENS, HALF), BF16)] * 2,
        in_specs=[vmem()] * 4 + [hbm() if at_edge else vmem()] + [hbm()] * 2,
        out_specs=[vmem()] * 2,
        scratch_shapes=scratch + [pltpu.SemaphoreType.DMA((6,))],
        compiler_params=pltpu.CompilerParams(vmem_limit_bytes=VMEM_LIMIT),
        name="second_layer_edge" if at_edge else "second_layer_side",
    )(halo, own, gains, order, proj, *far)


def swap(value):
    return lax.ppermute(value, "section", [(0, 1), (1, 0)])


def device_number(section, lat, lon):
    return (section * lax.axis_size("lat") + lat) * lax.axis_size("lon") + lon


def across(value):
    lats, lons = lax.axis_size("lat"), lax.axis_size("lon")
    pairs = []
    for lat in range(lats - 1):
        for lon in range(lons):
            south, north = device_number(1, lat, lon), device_number(0, lat + 1, lon)
            pairs += [(south, north), (north, south)]
    return lax.ppermute(value, ALL_AXES, pairs)


def on_device(
    level_tokens, enc_query, enc_weights, attn_proj, expand, contract, gains,
):
    section = lax.axis_index("section")
    pieces, *weights = encode(level_tokens, enc_query, enc_weights, expand, contract)
    own = lax.all_to_all(
        pieces.reshape(64, CHUNK, 128), ("lat", "lon"), split_axis=0, concat_axis=0, tiled=True
    )
    other = swap(own)
    rows = 64 * CHUNK
    edge, side = first_layer(
        own.reshape(rows, 128), other.reshape(rows, 128), enc_query, gains, attn_proj,
        weights,
    )
    far = across(edge)
    near = swap(side)
    order = jnp.asarray(order_table(), BF16)
    keep_side, send_side = second_layer(
        False, near, side, gains, order, attn_proj, expand, contract
    )
    got_side = swap(send_side)
    keep_edge, send_edge = second_layer(
        True, far, edge, gains, order, attn_proj, expand, contract
    )
    got_edge = swap(send_edge)
    first = section == 0
    out = jnp.concatenate(
        [
            jnp.where(first, keep_edge, got_edge),
            jnp.where(first, keep_side, got_side),
            jnp.where(first, got_side, keep_side),
            jnp.where(first, got_edge, keep_edge),
        ],
        axis=0,
    )
    return out.reshape(1, 8, LATENTS, 24, HALF).transpose(0, 1, 3, 2, 4)


def solution(mesh):
    return jax.shard_map(
        on_device,
        mesh=mesh,
        in_specs=(P(None, None, "lat", None, "lon", None, None), P(), P(), P(), P(), P(), P()),
        out_specs=P(None, "lat", "lon", None, "section"),
        check_vma=False,
    )
```

time: 93.3 us -> 59.1 us (0.63)
  waiting for transfers between devices: 16.4 us -> 3.78 us
  Pallas kernels: 34.7 us -> 24.1 us
  local copies, waits for them, and re-layouts: 8.68 us -> 0.03 us
  starting transfers between devices: 12.5 us -> 8.04 us
  blocking collectives: 19.3 us -> 21.4 us
    ppermute x4 -> x1, waiting for transfers between devices: 13.5 us -> 0.83 us  [across(): return lax.ppermute(value, ALL_AXES, pairs)]
    pallas_call x3 -> x4, Pallas kernels: 34.7 us -> 24.1 us  [the longest x2 9.15 us: second_layer(): pl.pallas_call(edge_kernel if at_edge else side_kernel, out_shape=[jax.Sh...]
    unnamed x13 -> x12, local copies, waits for them, and re-layouts: 5.85 us -> 0.03 us
    ppermute x4 -> x1, starting transfers between devices: 9.78 us -> 4.48 us  [across(): return lax.ppermute(value, ALL_AXES, pairs)]
    all_to_all x1, blocking collectives: 19.3 us -> 21.4 us  [on_device(): lax.all_to_all(pieces.reshape(64, CHUNK, 128), ('lat', 'lon'), split_axis...]
    slice x4 -> x0, local copies, waits for them, and re-layouts: 1.94 us -> none  [the longest x1 1 us: on_device(): below = move_rows(x[:TOKENS], -1)]
    ppermute x2 -> x4, starting transfers between devices: 2.7 us -> 3.56 us  [swap(): return lax.ppermute(value, 'section', [(0, 1), (1, 0)])]
    ppermute x2 -> x4, waiting for transfers between devices: 2.91 us -> 2.95 us  [swap(): return lax.ppermute(value, 'section', [(0, 1), (1, 0)])]
  transfers between devices with their start and end apart: 6 -> 5, of which waited for: 5 -> 3; matrix products, arithmetic and copies ran while one was open for 1% -> 0% of each run, Pallas kernels for 0% -> 16%
where the time goes in v1:
time: 59.1 us; the launch traced here: 58.2 us
  Pallas kernels  24.1 us (41%)
  blocking collectives  21.4 us (36%)
  starting transfers between devices  8.04 us (14%)
  waiting for transfers between devices  3.78 us (6%)
  other arithmetic  0.77 us (1%)
    all_to_all x1, blocking collectives, on_device(): lax.all_to_all(pieces.reshape(64, CHUNK, 128), ('lat', 'lon'), split_axis...  21.4 us
    pallas_call x2, Pallas kernels, second_layer(): pl.pallas_call(edge_kernel if at_edge else side_kernel, out_shape=[jax.Sh...  9.15 us
    pallas_call x1, Pallas kernels, first_layer(): pl.pallas_call(first_kernel, out_shape=[jax.ShapeDtypeStruct((WIDE, D), B...  7.86 us
    pallas_call x1, Pallas kernels, encode(): pl.pallas_call(encode_kernel, grid=(steps,), out_shape=[jax.ShapeDtypeStr...  7.1 us
    ppermute x1, starting transfers between devices, across(): return lax.ppermute(value, ALL_AXES, pairs)  4.48 us
    ppermute x4, starting transfers between devices, swap(): return lax.ppermute(value, 'section', [(0, 1), (1, 0)])  3.56 us
    ppermute x4, waiting for transfers between devices, swap(): return lax.ppermute(value, 'section', [(0, 1), (1, 0)])  2.95 us
  transfers between devices with their start and end apart: 5, of which 3 were waited for; matrix products, arithmetic and copies ran while one was open for 0% of the time, Pallas kernels for 16%

profile of v1, /device:TPU:7, one launch (start us, length us, event | category | flops | bytes accessed | tf_op | source)
XLA Modules:
  0.0 58.2 jit_solution(6527559624244498353)
XLA Ops:
  0.0 0.0 copy-start.4
  0.0 0.0 copy-start.5
  0.0 7.1 %encode_levels.1 = (bf16[2560,128]{1,0:T(8,128)(2,1)S(1)}, bf16[512,512]{1,0:T(8,128)(2,1)S(1)}, bf16[512,2048]{1,0:T(8,128)(2,1)S(1)}, bf16[2048,512]{1,0:T(8,128)(2,1)S(1)}) custom-call(bf16[2496,512]{1,0:T(8,128)(2,1)} %bitcast.12, bf16[3,512]{1,0:T(4,128)(2,1)} %query_ref.3, bf16[4,512,512]{2,1,0:T(8,128)(2,1)} %enc_hbm.1, ...), custom_call_target="tpu_custom_call" | custom-call | tf_op jit(solution)/shard_map/encode_levels/pallas_call | solution.py:272
  7.1 21.4 %all_to_all.5 = bf16[64,40,128]{2,1,0:T(8,128)(2,1)S(1)} all-to-all(bf16[64,40,128]{2,1,0:T(8,128)(2,1)S(1)} %bitcast.11), channel_id=1, replica_groups=mesh['section'=2,'lat'=8,'lon'=8] {'lat','lon'}, dimensions={0} | all-to-all | bytes 1310720 | tf_op jit(solution)/shard_map/all_to_all | solution.py:469
  28.5 2.9 %collective-permute-start = (bf16[64,40,128]{2,1,0:T(8,128)(2,1)S(1)}, bf16[64,40,128]{2,1,0:T(8,128)(2,1)S(1)}, u32[]{:S(2)}, u32[]{:S(2)}) collective-permute-start(bf16[64,40,128]{2,1,0:T(8,128)(2,1)S(1)} %all_to_all.5), channel_id=1, source_target_pairs={{0,64},{64,0},{1,65},{65,1},{2,66},{66,2},{3,67},{67,3},{4,68},{68... | collective-permute-start | bytes 1966088 | tf_op jit(solution)/shard_map/ppermute | solution.py:447
  31.4 1.7 %collective-permute-done = bf16[64,40,128]{2,1,0:T(8,128)(2,1)S(1)} collective-permute-done((bf16[64,40,128]{2,1,0:T(8,128)(2,1)S(1)}, bf16[64,40,128]{2,1,0:T(8,128)(2,1)S(1)}, u32[]{:S(2)}, u32[]{:S(2)}) %collective-permute-start) | collective-permute-done | bytes 655392 | tf_op jit(solution)/shard_map/ppermute | solution.py:447
  33.2 0.0 copy-done
  33.2 0.0 copy-done.1
  33.2 0.0 copy-done.2
  33.2 0.0 copy-done.4
  33.2 0.0 copy-done.5
  33.2 0.0 copy-start.3
  33.2 7.9 %first_layer.1 = (bf16[216,512]{1,0:T(8,128)(2,1)S(1)}, bf16[216,512]{1,0:T(8,128)(2,1)S(1)}) custom-call(bf16[2560,128]{1,0:T(8,128)(2,1)S(1)} %bitcast.9, bf16[2560,128]{1,0:T(8,128)(2,1)S(1)} %bitcast.10, bf16[3,512]{1,0:T(4,128)(2,1)S(1)} %copy-done.5, f32[2,2,512]{2,1,0:T(2,128)S(1)} %copy-done.4, bf16[2,288,640]{2,1,0:T(8,128)(2,1)S(1)} %copy-done.1, ...), custom_call_target="tpu_custom_call" | custom-call | tf_op jit(solution)/shard_map/first_layer/pallas_call | solution.py:353
  41.1 0.5 collective-permute-start.3
  41.5 4.5 %collective-permute-start.1 = (bf16[216,512]{1,0:T(8,128)(2,1)S(1)}, bf16[216,512]{1,0:T(8,128)(2,1)S(1)}, u32[]{:S(2)}, u32[]{:S(2)}) collective-permute-start(bf16[216,512]{1,0:T(8,128)(2,1)S(1)} %get-tuple-element.19.own_ref), channel_id=1, source_target_pairs={{64,8},{8,64},{65,9},{9,65},{66,10},{10,66},{67,11},{11,67},{68,12... | collective-permute-start | bytes 663560 | tf_op jit(solution)/shard_map/ppermute | solution.py:461
  46.0 0.0 collective-permute-done.3.halo_ref
  46.0 3.9 %second_layer_side.1 = (bf16[144,256]{1,0:T(8,128)(2,1)S(1)}, bf16[144,256]{1,0:T(8,128)(2,1)S(1)}) custom-call(bf16[216,512]{1,0:T(8,128)(2,1)S(1)} %collective-permute-done.3.halo_ref, bf16[216,512]{1,0:T(8,128)(2,1)S(1)} %get-tuple-element.22.own_ref, f32[2,2,512]{2,1,0:T(2,128)S(1)} %copy-done.4, bf16[144,160]{1,0:T(8,128)(2,1)S(1)} %copy-done.3, ...), custom_call_target="tpu_custom_call" | custom-call | tf_op jit(solution)/shard_map/second_layer_side/pallas_call | solution.py:435
  50.0 0.1 collective-permute-start.4
  50.1 0.8 %collective-permute-done.1.halo_ref = bf16[216,512]{1,0:T(8,128)(2,1)S(1)} collective-permute-done((bf16[216,512]{1,0:T(8,128)(2,1)S(1)}, bf16[216,512]{1,0:T(8,128)(2,1)S(1)}, u32[]{:S(2)}, u32[]{:S(2)}) %collective-permute-start.1) | collective-permute-done | bytes 221216 | tf_op jit(solution)/shard_map/ppermute | solution.py:461
  50.9 5.2 %second_layer_edge.1 = (bf16[144,256]{1,0:T(8,128)(2,1)S(1)}, bf16[144,256]{1,0:T(8,128)(2,1)S(1)}) custom-call(bf16[216,512]{1,0:T(8,128)(2,1)S(1)} %collective-permute-done.1.halo_ref, bf16[216,512]{1,0:T(8,128)(2,1)S(1)} %get-tuple-element.19.own_ref, f32[2,2,512]{2,1,0:T(2,128)S(1)} %copy-done.4, bf16[144,160]{1,0:T(8,128)(2,1)S(1)} %copy-done.3, ...), custom_call_target="tpu_custom_call" | custom-call | tf_op jit(solution)/shard_map/second_layer_edge/pallas_call | solution.py:435
  56.1 0.1 collective-permute-start.2
  56.2 0.0 collective-permute-done.4
  56.3 1.2 %collective-permute-done.2 = bf16[144,256]{1,0:T(8,128)(2,1)S(1)} collective-permute-done((bf16[144,256]{1,0:T(8,128)(2,1)S(1)}, bf16[144,256]{1,0:T(8,128)(2,1)S(1)}, u32[]{:S(2)}, u32[]{:S(2)}) %collective-permute-start.2) | collective-permute-done | bytes 73760 | tf_op jit(solution)/shard_map/ppermute | solution.py:447
  57.5 0.7 %pad_maximum_fusion = bf16[576,256]{1,0:T(8,128)(2,1)} fusion(bf16[144,256]{1,0:T(8,128)(2,1)S(1)} %get-tuple-element.26, bf16[144,256]{1,0:T(8,128)(2,1)S(1)} %get-tuple-element.28, bf16[144,256]{1,0:T(8,128)(2,1)S(1)} %get-tuple-element.27, bf16[144,256]{1,0:T(8,128)(2,1)S(1)} %get-tuple-element.25), kind=kLoop, calls=%fused_computation | loop fusion | flops 1179648 | bytes 589824 | tf_op jit(solution)/shard_map/concatenate | solution.py:490
  (6 shorter events, 0.0 us)
Async XLA Ops:
  0.0 33.2 %copy-start = (bf16[2,4,512,512]{3,2,1,0:T(8,128)(2,1)S(1)}, bf16[2,4,512,512]{3,2,1,0:T(8,128)(2,1)}, u32[]{:S(2)}) copy-start(bf16[2,4,512,512]{3,2,1,0:T(8,128)(2,1)} %proj_ref.3) | copy-start | bytes 12582916
  0.0 33.2 %copy-start.1 = (bf16[2,288,640]{2,1,0:T(8,128)(2,1)S(1)}, bf16[2,288,640]{2,1,0:T(8,128)(2,1)}, u32[]{:S(2)}) copy-start(bf16[2,288,640]{2,1,0:T(8,128)(2,1)} %constant.20.clone.compact_ref) | copy-start | bytes 2211844
  0.0 33.2 %copy-start.2 = (bf16[2,216,432]{2,1,0:T(8,128)(2,1)S(1)}, bf16[2,216,432]{2,1,0:T(8,128)(2,1)}, u32[]{:S(2)}) copy-start(bf16[2,216,432]{2,1,0:T(8,128)(2,1)} %constant.21.clone.bands_ref) | copy-start | bytes 1119748
  0.0 33.2 %copy-start.4 = (f32[2,2,512]{2,1,0:T(2,128)S(1)}, f32[2,2,512]{2,1,0:T(2,128)}, u32[]{:S(2)}) copy-start(f32[2,2,512]{2,1,0:T(2,128)} %gain_ref.5) | copy-start | bytes 24580
  0.0 33.2 %copy-start.5 = (bf16[3,512]{1,0:T(4,128)(2,1)S(1)}, bf16[3,512]{1,0:T(4,128)(2,1)}, u32[]{:S(2)}) copy-start(bf16[3,512]{1,0:T(4,128)(2,1)} %query_ref.3) | copy-start | bytes 9220
  28.5 4.7 %collective-permute-start = (bf16[64,40,128]{2,1,0:T(8,128)(2,1)S(1)}, bf16[64,40,128]{2,1,0:T(8,128)(2,1)S(1)}, u32[]{:S(2)}, u32[]{:S(2)}) collective-permute-start(bf16[64,40,128]{2,1,0:T(8,128)(2,1)S(1)} %all_to_all.5), channel_id=1, source_target_pairs={{0,64},{64,0},{1,65},{65,1},{2,66},{66,2},{3,67},{67,3},{4,68},{68... | collective-permute-start | bytes 1966088 | tf_op jit(solution)/shard_map/ppermute | solution.py:447
  33.2 12.8 %copy-start.3 = (bf16[144,160]{1,0:T(8,128)(2,1)S(1)}, bf16[144,160]{1,0:T(8,128)(2,1)}, u32[]{:S(2)}) copy-start(bf16[144,160]{1,0:T(8,128)(2,1)} %constant.22.clone.order_ref) | copy-start | bytes 138244
  41.1 4.9 %collective-permute-start.3 = (bf16[216,512]{1,0:T(8,128)(2,1)S(1)}, bf16[216,512]{1,0:T(8,128)(2,1)S(1)}, u32[]{:S(2)}, u32[]{:S(2)}) collective-permute-start(bf16[216,512]{1,0:T(8,128)(2,1)S(1)} %get-tuple-element.22.own_ref), channel_id=1, source_target_pairs={{0,64},{64,0},{1,65},{65,1},{2,66},{66,2},{3,67},{67,3},{4,68},{68... | collective-permute-start | bytes 663560 | tf_op jit(solution)/shard_map/ppermute | solution.py:447
  41.5 9.3 %collective-permute-start.1 = (bf16[216,512]{1,0:T(8,128)(2,1)S(1)}, bf16[216,512]{1,0:T(8,128)(2,1)S(1)}, u32[]{:S(2)}, u32[]{:S(2)}) collective-permute-start(bf16[216,512]{1,0:T(8,128)(2,1)S(1)} %get-tuple-element.19.own_ref), channel_id=1, source_target_pairs={{64,8},{8,64},{65,9},{9,65},{66,10},{10,66},{67,11},{11,67},{68,12... | collective-permute-start | bytes 663560 | tf_op jit(solution)/shard_map/ppermute | solution.py:461
  50.0 6.3 %collective-permute-start.4 = (bf16[144,256]{1,0:T(8,128)(2,1)S(1)}, bf16[144,256]{1,0:T(8,128)(2,1)S(1)}, u32[]{:S(2)}, u32[]{:S(2)}) collective-permute-start(bf16[144,256]{1,0:T(8,128)(2,1)S(1)} %get-tuple-element.24), channel_id=1, source_target_pairs={{0,64},{64,0},{1,65},{65,1},{2,66},{66,2},{3,67},{67,3},{4,68},{68... | collective-permute-start | bytes 221192 | tf_op jit(solution)/shard_map/ppermute | solution.py:447
  56.1 1.3 %collective-permute-start.2 = (bf16[144,256]{1,0:T(8,128)(2,1)S(1)}, bf16[144,256]{1,0:T(8,128)(2,1)S(1)}, u32[]{:S(2)}, u32[]{:S(2)}) collective-permute-start(bf16[144,256]{1,0:T(8,128)(2,1)S(1)} %get-tuple-element.21), channel_id=1, source_target_pairs={{0,64},{64,0},{1,65},{65,1},{2,66},{66,2},{3,67},{67,3},{4,68},{68... | collective-permute-start | bytes 221192 | tf_op jit(solution)/shard_map/ppermute | solution.py:447

commit v2 on v1

--- a/solution.py
+++ b/solution.py
@@ -36,25 +36,21 @@
     return out
 
 
-def encoder_tables():
-    expand = one_hot(
-        128, LATENTS * HALF,
-        [
-            (l * GROUP + h, l * HALF + h * HEAD + e)
-            for l in range(LATENTS) for h in range(GROUP) for e in range(HEAD)
-        ],
-    )
-    scatter = [
+def scatter_table():
+    return np.stack([
         one_hot(
-            8 * CHUNK, 72,
+            8 * CHUNK, 144,
             [
-                (b * CHUNK + half * 18 + d * 9 + w * 3 + l, l * 24 + w * 8 + (b + d * side) % 8)
+                (
+                    b * CHUNK + half * 18 + d * 9 + w * 3 + l,
+                    half * 72 + l * 24 + w * 8 + (b + d * side) % 8,
+                )
+                for half in range(2)
                 for b in range(8) for d in range(2) for w in range(3) for l in range(3)
             ],
         )
-        for side in (1, -1) for half in range(2)
-    ]
-    return expand, np.stack(scatter)
+        for side in (1, -1)
+    ])
 
 
 def compact_table():
@@ -202,54 +198,70 @@
 
 
 def encode_kernel(
-    x_ref, query_ref, w_ref, expand_ref, scatter_ref, enc_hbm, in_hbm, out_hbm,
-    out_ref, enc_next, in_next, out_next, keys, sems,
+    x_hbm, query_hbm, w_hbm, scatter_hbm, in_hbm, out_hbm,
+    out_ref, enc_next, in_next, out_next, x, query, w, scatter, sems, next_sems,
 ):
+    section = lax.axis_index("section")
     side = lax.axis_index("lon") // 4
+    half = pl.ds(pl.multiple_of(section * HALF, HALF), HALF)
+    steps = x.shape[0]
+    rows = x.shape[1]
+    count = rows // (LEVELS * 24)
+    blocks = [x_hbm.at[pl.ds(i * rows, rows), :] for i in range(steps)]
     copies = fetch(
-        (enc_hbm.at[3], in_hbm.at[0], out_hbm.at[0]), (enc_next, in_next, out_next), sems
-    )
-
-    @pl.when(pl.program_id(0) == pl.num_programs(0) - 2)
-    def _():
-        for copy in copies:
-            copy.start()
-
-    @pl.when(pl.program_id(0) == 0)
-    def _():
-        query = jnp.concatenate([query_ref[...], jnp.zeros((5, D), BF16)], axis=0)
-        latent = dot(query, w_ref[0]).astype(BF16).astype(F32)
-        turned = latent.T
-        col = lax.broadcasted_iota(jnp.int32, (HALF, 128), 1)
-        head = lax.broadcasted_iota(jnp.int32, (HALF, 128), 0) // HEAD
-        spread = jnp.zeros((HALF, 128), F32)
+        [query_hbm] + [w_hbm.at[i, :, half] for i in range(3)]
+        + [scatter_hbm.at[side]] + blocks,
+        [query] + [w.at[i] for i in range(3)] + [scatter] + [x.at[i] for i in range(steps)],
+        sems,
+    )
+    later = fetch(
+        (w_hbm.at[3], in_hbm.at[0], out_hbm.at[0]), (enc_next, in_next, out_next), next_sems
+    )
+    for copy in copies:
+        copy.start()
+    for copy in copies[:3]:
+        copy.wait()
+    padded = jnp.concatenate([query[...], jnp.zeros((5, D), BF16)], axis=0)
+    turned = dot(padded, w[0]).astype(BF16).astype(F32).T
+    col = lax.broadcasted_iota(jnp.int32, (HALF, 128), 1)
+    head = lax.broadcasted_iota(jnp.int32, (HALF, 128), 0) // HEAD
+    spread = jnp.zeros((HALF, 128), F32)
+    for l in range(LATENTS):
+        spread = jnp.where(col == l * GROUP + head, turned[:, l : l + 1], spread)
+    keys = (dot(w[1], spread.astype(BF16)) * SCALE).astype(BF16)
+    row = lax.broadcasted_iota(jnp.int32, (128, HALF), 0)
+    lane = lax.broadcasted_iota(jnp.int32, (128, HALF), 1) // HEAD
+    expand = [
+        jnp.where(row == l * GROUP + lane, 1.0, 0.0).astype(BF16) for l in range(LATENTS)
+    ]
+    for copy in copies[3:5]:
+        copy.wait()
+    for step in range(steps):
+        copies[5 + step].wait()
+        if step == 1:
+            for copy in later:
+                copy.start()
+        block = x[step]
+        value = dot(block, w[2])
+        scores = dot(block, keys).reshape(count * 3, LEVELS, 8, 128)
+        expd = jnp.exp2(scores - jnp.max(scores, axis=1, keepdims=True))
+        share = (expd / jnp.sum(expd, axis=1, keepdims=True)).reshape(rows, 128).astype(BF16)
+        mixed = []
         for l in range(LATENTS):
-            spread = jnp.where(col == l * GROUP + head, turned[:, l : l + 1], spread)
-        keys[...] = (dot(w_ref[1], spread.astype(BF16)) * SCALE).astype(BF16)
-
-    x = x_ref[...]
-    rows = x.shape[0]
-    count = rows // (LEVELS * 24)
-    value = dot(x, w_ref[2])
-    scores = dot(x, keys[...]).reshape(count * 3, LEVELS, 8, 128)
-    expd = jnp.exp2(scores - jnp.max(scores, axis=1, keepdims=True))
-    share = (expd / jnp.sum(expd, axis=1, keepdims=True)).reshape(rows, 128).astype(BF16)
-    mixed = []
-    for l in range(LATENTS):
-        weighted = dot(share, expand_ref[:, l * HALF : (l + 1) * HALF]) * value
-        mixed.append(jnp.sum(weighted.reshape(count * 3, LEVELS, 8, HALF), axis=1))
-    for a in range(count):
-        part = [m[3 * a : 3 * a + 3].reshape(24, HALF) for m in mixed]
-        part = jnp.concatenate(part, axis=0).astype(BF16)
-        out_ref[a * 8 * CHUNK : (a + 1) * 8 * CHUNK, :] = (
-            dot(scatter_ref[2 * side], part[:, :128])
-            + dot(scatter_ref[2 * side + 1], part[:, 128:])
-        ).astype(BF16)
-
-    @pl.when(pl.program_id(0) == pl.num_programs(0) - 1)
-    def _():
-        for copy in copies:
-            copy.wait()
+            weighted = dot(share, expand[l]) * value
+            mixed.append(jnp.sum(weighted.reshape(count * 3, LEVELS, 8, HALF), axis=1))
+        pairs = []
+        for a in range(count):
+            part = [m[3 * a : 3 * a + 3].reshape(24, HALF) for m in mixed]
+            pairs.append(
+                jnp.concatenate([p[:, :128] for p in part] + [p[:, 128:] for p in part], axis=0)
+            )
+        pieces = dot(scatter[...], jnp.concatenate(pairs, axis=1).astype(BF16)).astype(BF16)
+        for a in range(count):
+            start = (step * count + a) * 8 * CHUNK
+            out_ref[start : start + 8 * CHUNK, :] = pieces[:, a * 128 : (a + 1) * 128]
+    for copy in later:
+        copy.wait()
 
 
 def vmem():
@@ -266,33 +278,32 @@
 
 def encode(level_tokens, enc_query, enc_weights, expand, contract):
     source = level_tokens.transpose(0, 1, 2, 4, 5, 3, 6).reshape(-1, D)
-    spread, scatter = encoder_tables()
+    scatter = scatter_table()
     block = 2 * 24 * LEVELS
     steps = source.shape[0] // block
     return pl.pallas_call(
         encode_kernel,
-        grid=(steps,),
         out_shape=[
             jax.ShapeDtypeStruct((steps * 16 * CHUNK, 128), BF16),
             pltpu.VMEM((D, D), BF16),
             pltpu.VMEM((D, FF), BF16),
             pltpu.VMEM((FF, D), BF16),
         ],
-        in_specs=[
-            pl.BlockSpec((block, D), lambda i: (i, 0)),
-            pl.BlockSpec((LATENTS, D), lambda i: (0, 0)),
-            pl.BlockSpec((3, D, HALF), lambda i: (0, 0, lax.axis_index("section"))),
-            pl.BlockSpec(spread.shape, lambda i: (0, 0)),
-            pl.BlockSpec(scatter.shape, lambda i: (0, 0, 0)),
-        ] + [hbm()] * 3,
-        out_specs=[pl.BlockSpec((16 * CHUNK, 128), lambda i: (i, 0))] + [hbm()] * 3,
-        scratch_shapes=[pltpu.VMEM((D, 128), BF16), pltpu.SemaphoreType.DMA((3,))],
+        in_specs=[hbm()] * 6,
+        out_specs=[vmem()] + [hbm()] * 3,
+        scratch_shapes=[
+            pltpu.VMEM((steps, block, D), BF16),
+            pltpu.VMEM((LATENTS, D), BF16),
+            pltpu.VMEM((3, D, HALF), BF16),
+            pltpu.VMEM(scatter.shape[1:], BF16),
+            pltpu.SemaphoreType.DMA((5 + steps,)),
+            pltpu.SemaphoreType.DMA((3,)),
+        ],
         compiler_params=pltpu.CompilerParams(vmem_limit_bytes=VMEM_LIMIT),
         name="encode_levels",
     )(
         *in_hbm_space(
-            source, enc_query, enc_weights, jnp.asarray(spread, BF16), jnp.asarray(scatter, BF16),
-            enc_weights, expand, contract,
+            source, enc_query, enc_weights, jnp.asarray(scatter, BF16), expand, contract
         )
     )
 
@@ -362,24 +373,22 @@
 
 def side_kernel(
     halo_ref, own_ref, gain_ref, order_ref, proj_ref, in_hbm, out_hbm,
+    keep_ref, send_ref, proj_next, w_in, w_out, sems,
+):
+    proj = proj_ref.at[1]
+    copies = fetch((in_hbm.at[1], out_hbm.at[1], proj), (w_in, w_out, proj_next), sems)
+    second(
+        False, copies, halo_ref, own_ref, gain_ref, order_ref, proj, w_in, w_out,
+        keep_ref, send_ref,
+    )
+    copies[2].wait()
+
+
+def edge_kernel(
+    halo_ref, own_ref, gain_ref, order_ref, proj, in_hbm, out_hbm,
     keep_ref, send_ref, w_in, w_out, sems,
 ):
     copies = fetch((in_hbm.at[1], out_hbm.at[1]), (w_in, w_out), sems)
-    second(
-        False, copies, halo_ref, own_ref, gain_ref, order_ref, proj_ref.at[1], w_in, w_out,
-        keep_ref, send_ref,
-    )
-
-
-def edge_kernel(
-    halo_ref, own_ref, gain_ref, order_ref, proj_hbm, in_hbm, out_hbm,
-    keep_ref, send_ref, w_in, w_out, proj, sems,
-):
-    copies = fetch(
-        [proj_hbm.at[1, i] for i in (1, 2, 0, 3)] + [in_hbm.at[1], out_hbm.at[1]],
-        [proj.at[i] for i in (1, 2, 0, 3)] + [w_in, w_out],
-        sems,
-    )
     second(
         True, copies, halo_ref, own_ref, gain_ref, order_ref, proj, w_in, w_out,
         keep_ref, send_ref,
@@ -401,8 +410,6 @@
         part = slice(72 * c, 72 * (c + 1))
         keys += [halo[part], own[part]]
     keys = jnp.concatenate(keys, axis=0).astype(BF16)
-    for copy in copies[:-2]:
-        copy.wait()
     q = dot(own[32:192].astype(BF16), proj[0]) * SCALE
     k = dot(keys, proj[1]).astype(BF16)
     v = dot(keys, proj[2]).astype(BF16)
@@ -418,7 +425,7 @@
     before = dot(order_ref[...], own_ref[32:192, :])
     middle = (before + dot(mixed, proj[3]).astype(BF16).astype(F32)).astype(BF16).astype(F32)
     flat = normed(middle, gain_ref[1, 1:2, :])
-    for copy in copies[-2:]:
+    for copy in copies[:2]:
         copy.wait()
     done = (middle + feed_forward(flat, w_in, w_out)).astype(BF16)
     low, high = done[:, :HALF], done[:, HALF:]
@@ -427,20 +434,20 @@
 
 
 def second_layer(at_edge, halo, own, gains, order, proj, expand, contract):
-    far = in_hbm_space(expand, contract)
-    scratch = [pltpu.VMEM((D, FF), BF16), pltpu.VMEM((FF, D), BF16)]
-    if at_edge:
-        (proj,) = in_hbm_space(proj)
-        scratch.append(pltpu.VMEM((4, D, D), BF16))
+    passed = [] if at_edge else [pltpu.VMEM(proj.shape[1:], BF16)]
     return pl.pallas_call(
         edge_kernel if at_edge else side_kernel,
-        out_shape=[jax.ShapeDtypeStruct((TOKENS, HALF), BF16)] * 2,
-        in_specs=[vmem()] * 4 + [hbm() if at_edge else vmem()] + [hbm()] * 2,
-        out_specs=[vmem()] * 2,
-        scratch_shapes=scratch + [pltpu.SemaphoreType.DMA((6,))],
+        out_shape=[jax.ShapeDtypeStruct((TOKENS, HALF), BF16)] * 2 + passed,
+        in_specs=[vmem()] * 5 + [hbm()] * 2,
+        out_specs=[vmem()] * 2 + [hbm()] * len(passed),
+        scratch_shapes=[
+            pltpu.VMEM((D, FF), BF16),
+            pltpu.VMEM((FF, D), BF16),
+            pltpu.SemaphoreType.DMA((3,)),
+        ],
         compiler_params=pltpu.CompilerParams(vmem_limit_bytes=VMEM_LIMIT),
         name="second_layer_edge" if at_edge else "second_layer_side",
-    )(halo, own, gains, order, proj, *far)
+    )(halo, own, gains, order, proj, *in_hbm_space(expand, contract))
 
 
 def swap(value):
@@ -478,12 +485,12 @@
     far = across(edge)
     near = swap(side)
     order = jnp.asarray(order_table(), BF16)
-    keep_side, send_side = second_layer(
+    keep_side, send_side, proj = second_layer(
         False, near, side, gains, order, attn_proj, expand, contract
     )
     got_side = swap(send_side)
     keep_edge, send_edge = second_layer(
-        True, far, edge, gains, order, attn_proj, expand, contract
+        True, far, edge, gains, order, proj, expand, contract
     )
     got_edge = swap(send_edge)
     first = section == 0

time: 59.1 us -> 56.8 us (0.961)
  Pallas kernels: 24.1 us -> 22.1 us
    pallas_call x2, Pallas kernels: 9.15 us -> 8.06 us  [second_layer(): pl.pallas_call(edge_kernel if at_edge else side_kernel, out_shape=[jax.Sh...]
    pallas_call x1, Pallas kernels: 7.1 us -> 6.15 us  [encode(): pl.pallas_call(encode_kernel, out_shape=[jax.ShapeDtypeStruct((steps * 16...]
  transfers between devices with their start and end apart: 5 -> 5, of which waited for: 3 -> 3; matrix products, arithmetic and copies ran while one was open for 0% -> 0% of each run, Pallas kernels for 16% -> 14%
where the time goes in v2:
time: 56.8 us; the launch traced here: 56.1 us
  Pallas kernels  22.1 us (39%)
  blocking collectives  21.4 us (38%)
  starting transfers between devices  8.01 us (14%)
  waiting for transfers between devices  3.7 us (7%)
  other arithmetic  0.77 us (1%)
    all_to_all x1, blocking collectives, on_device(): lax.all_to_all(pieces.reshape(64, CHUNK, 128), ('lat', 'lon'), split_axis...  21.4 us
    pallas_call x2, Pallas kernels, second_layer(): pl.pallas_call(edge_kernel if at_edge else side_kernel, out_shape=[jax.Sh...  8.06 us
    pallas_call x1, Pallas kernels, first_layer(): pl.pallas_call(first_kernel, out_shape=[jax.ShapeDtypeStruct((WIDE, D), B...  7.86 us
    pallas_call x1, Pallas kernels, encode(): pl.pallas_call(encode_kernel, out_shape=[jax.ShapeDtypeStruct((steps * 16...  6.15 us
    ppermute x1, starting transfers between devices, across(): return lax.ppermute(value, ALL_AXES, pairs)  4.42 us
    ppermute x4, starting transfers between devices, swap(): return lax.ppermute(value, 'section', [(0, 1), (1, 0)])  3.59 us
    ppermute x4, waiting for transfers between devices, swap(): return lax.ppermute(value, 'section', [(0, 1), (1, 0)])  2.95 us
  transfers between devices with their start and end apart: 5, of which 3 were waited for; matrix products, arithmetic and copies ran while one was open for 0% of the time, Pallas kernels for 14%

profile of v2, /device:TPU:7, one launch (start us, length us, event | category | flops | bytes accessed | tf_op | source)
XLA Modules:
  0.0 56.1 jit_solution(9643073654360716687)
XLA Ops:
  0.0 0.0 copy-start.4
  0.0 0.0 copy-start.5
  0.0 6.1 %encode_levels.1 = (bf16[2560,128]{1,0:T(8,128)(2,1)S(1)}, bf16[512,512]{1,0:T(8,128)(2,1)S(1)}, bf16[512,2048]{1,0:T(8,128)(2,1)S(1)}, bf16[2048,512]{1,0:T(8,128)(2,1)S(1)}) custom-call(bf16[2496,512]{1,0:T(8,128)(2,1)} %bitcast.12, bf16[3,512]{1,0:T(4,128)(2,1)} %query_ref.1, bf16[4,512,512]{2,1,0:T(8,128)(2,1)} %w_hbm.1, ...), custom_call_target="tpu_custom_call" | custom-call | tf_op jit(solution)/shard_map/encode_levels/pallas_call | solution.py:284
  6.2 21.4 %all_to_all.5 = bf16[64,40,128]{2,1,0:T(8,128)(2,1)S(1)} all-to-all(bf16[64,40,128]{2,1,0:T(8,128)(2,1)S(1)} %bitcast.11), channel_id=1, replica_groups=mesh['section'=2,'lat'=8,'lon'=8] {'lat','lon'}, dimensions={0} | all-to-all | bytes 1310720 | tf_op jit(solution)/shard_map/all_to_all | solution.py:476
  27.5 2.9 %collective-permute-start = (bf16[64,40,128]{2,1,0:T(8,128)(2,1)S(1)}, bf16[64,40,128]{2,1,0:T(8,128)(2,1)S(1)}, u32[]{:S(2)}, u32[]{:S(2)}) collective-permute-start(bf16[64,40,128]{2,1,0:T(8,128)(2,1)S(1)} %all_to_all.5), channel_id=1, source_target_pairs={{0,64},{64,0},{1,65},{65,1},{2,66},{66,2},{3,67},{67,3},{4,68},{68... | collective-permute-start | bytes 1966088 | tf_op jit(solution)/shard_map/ppermute | solution.py:454
  30.5 1.7 %collective-permute-done = bf16[64,40,128]{2,1,0:T(8,128)(2,1)S(1)} collective-permute-done((bf16[64,40,128]{2,1,0:T(8,128)(2,1)S(1)}, bf16[64,40,128]{2,1,0:T(8,128)(2,1)S(1)}, u32[]{:S(2)}, u32[]{:S(2)}) %collective-permute-start) | collective-permute-done | bytes 655392 | tf_op jit(solution)/shard_map/ppermute | solution.py:454
  32.2 0.0 copy-done
  32.2 0.0 copy-done.1
  32.2 0.0 copy-done.2
  32.2 0.0 copy-done.4
  32.2 0.0 copy-done.5
  32.2 0.0 copy-start.3
  32.2 7.9 %first_layer.1 = (bf16[216,512]{1,0:T(8,128)(2,1)S(1)}, bf16[216,512]{1,0:T(8,128)(2,1)S(1)}) custom-call(bf16[2560,128]{1,0:T(8,128)(2,1)S(1)} %bitcast.9, bf16[2560,128]{1,0:T(8,128)(2,1)S(1)} %bitcast.10, bf16[3,512]{1,0:T(4,128)(2,1)S(1)} %copy-done.5, f32[2,2,512]{2,1,0:T(2,128)S(1)} %copy-done.4, bf16[2,288,640]{2,1,0:T(8,128)(2,1)S(1)} %copy-done.1, ...), custom_call_target="tpu_custom_call" | custom-call | tf_op jit(solution)/shard_map/first_layer/pallas_call | solution.py:364
  40.1 0.5 collective-permute-start.2
  40.6 4.4 %collective-permute-start.1 = (bf16[216,512]{1,0:T(8,128)(2,1)S(1)}, bf16[216,512]{1,0:T(8,128)(2,1)S(1)}, u32[]{:S(2)}, u32[]{:S(2)}) collective-permute-start(bf16[216,512]{1,0:T(8,128)(2,1)S(1)} %get-tuple-element.20.own_ref), channel_id=1, source_target_pairs={{64,8},{8,64},{65,9},{9,65},{66,10},{10,66},{67,11},{11,67},{68,12... | collective-permute-start | bytes 663560 | tf_op jit(solution)/shard_map/ppermute | solution.py:468
  45.0 0.0 collective-permute-done.2.halo_ref
  45.0 4.0 %second_layer_side.1 = (bf16[144,256]{1,0:T(8,128)(2,1)S(1)}, bf16[144,256]{1,0:T(8,128)(2,1)S(1)}, bf16[4,512,512]{2,1,0:T(8,128)(2,1)S(1)}) custom-call(bf16[216,512]{1,0:T(8,128)(2,1)S(1)} %collective-permute-done.2.halo_ref, bf16[216,512]{1,0:T(8,128)(2,1)S(1)} %get-tuple-element.21.own_ref, f32[2,2,512]{2,1,0:T(2,128)S(1)} %copy-done.4, ...), custom_call_target="tpu_custom_call" | custom-call | tf_op jit(solution)/shard_map/second_layer_side/pallas_call | solution.py:438
  49.1 0.1 collective-permute-start.4
  49.2 0.8 %collective-permute-done.1.halo_ref = bf16[216,512]{1,0:T(8,128)(2,1)S(1)} collective-permute-done((bf16[216,512]{1,0:T(8,128)(2,1)S(1)}, bf16[216,512]{1,0:T(8,128)(2,1)S(1)}, u32[]{:S(2)}, u32[]{:S(2)}) %collective-permute-start.1) | collective-permute-done | bytes 221216 | tf_op jit(solution)/shard_map/ppermute | solution.py:468
  49.9 4.0 %second_layer_edge.1 = (bf16[144,256]{1,0:T(8,128)(2,1)S(1)}, bf16[144,256]{1,0:T(8,128)(2,1)S(1)}) custom-call(bf16[216,512]{1,0:T(8,128)(2,1)S(1)} %collective-permute-done.1.halo_ref, bf16[216,512]{1,0:T(8,128)(2,1)S(1)} %get-tuple-element.20.own_ref, f32[2,2,512]{2,1,0:T(2,128)S(1)} %copy-done.4, bf16[144,160]{1,0:T(8,128)(2,1)S(1)} %copy-done.3, ...), custom_call_target="tpu_custom_call" | custom-call | tf_op jit(solution)/shard_map/second_layer_edge/pallas_call | solution.py:438
  54.0 0.1 collective-permute-start.3
  54.1 0.0 collective-permute-done.4
  54.1 1.2 %collective-permute-done.3 = bf16[144,256]{1,0:T(8,128)(2,1)S(1)} collective-permute-done((bf16[144,256]{1,0:T(8,128)(2,1)S(1)}, bf16[144,256]{1,0:T(8,128)(2,1)S(1)}, u32[]{:S(2)}, u32[]{:S(2)}) %collective-permute-start.3) | collective-permute-done | bytes 73760 | tf_op jit(solution)/shard_map/ppermute | solution.py:454
  55.3 0.7 %pad_maximum_fusion = bf16[576,256]{1,0:T(8,128)(2,1)} fusion(bf16[144,256]{1,0:T(8,128)(2,1)S(1)} %get-tuple-element.28, bf16[144,256]{1,0:T(8,128)(2,1)S(1)} %get-tuple-element.30, bf16[144,256]{1,0:T(8,128)(2,1)S(1)} %get-tuple-element.29, bf16[144,256]{1,0:T(8,128)(2,1)S(1)} %get-tuple-element.27), kind=kLoop, calls=%fused_computation | loop fusion | flops 1179648 | bytes 589824 | tf_op jit(solution)/shard_map/concatenate | solution.py:497
  (6 shorter events, 0.0 us)
Async XLA Ops:
  0.0 32.2 %copy-start = (bf16[2,4,512,512]{3,2,1,0:T(8,128)(2,1)S(1)}, bf16[2,4,512,512]{3,2,1,0:T(8,128)(2,1)}, u32[]{:S(2)}) copy-start(bf16[2,4,512,512]{3,2,1,0:T(8,128)(2,1)} %proj_ref.3) | copy-start | bytes 12582916
  0.0 32.2 %copy-start.1 = (bf16[2,288,640]{2,1,0:T(8,128)(2,1)S(1)}, bf16[2,288,640]{2,1,0:T(8,128)(2,1)}, u32[]{:S(2)}) copy-start(bf16[2,288,640]{2,1,0:T(8,128)(2,1)} %constant.17.clone.compact_ref) | copy-start | bytes 2211844
  0.0 32.2 %copy-start.2 = (bf16[2,216,432]{2,1,0:T(8,128)(2,1)S(1)}, bf16[2,216,432]{2,1,0:T(8,128)(2,1)}, u32[]{:S(2)}) copy-start(bf16[2,216,432]{2,1,0:T(8,128)(2,1)} %constant.18.clone.bands_ref) | copy-start | bytes 1119748
  0.0 32.2 %copy-start.4 = (f32[2,2,512]{2,1,0:T(2,128)S(1)}, f32[2,2,512]{2,1,0:T(2,128)}, u32[]{:S(2)}) copy-start(f32[2,2,512]{2,1,0:T(2,128)} %gain_ref.5) | copy-start | bytes 24580
  0.0 32.2 %copy-start.5 = (bf16[3,512]{1,0:T(4,128)(2,1)S(1)}, bf16[3,512]{1,0:T(4,128)(2,1)}, u32[]{:S(2)}) copy-start(bf16[3,512]{1,0:T(4,128)(2,1)} %query_ref.1) | copy-start | bytes 9220
  27.5 4.7 %collective-permute-start = (bf16[64,40,128]{2,1,0:T(8,128)(2,1)S(1)}, bf16[64,40,128]{2,1,0:T(8,128)(2,1)S(1)}, u32[]{:S(2)}, u32[]{:S(2)}) collective-permute-start(bf16[64,40,128]{2,1,0:T(8,128)(2,1)S(1)} %all_to_all.5), channel_id=1, source_target_pairs={{0,64},{64,0},{1,65},{65,1},{2,66},{66,2},{3,67},{67,3},{4,68},{68... | collective-permute-start | bytes 1966088 | tf_op jit(solution)/shard_map/ppermute | solution.py:454
  32.2 12.8 %copy-start.3 = (bf16[144,160]{1,0:T(8,128)(2,1)S(1)}, bf16[144,160]{1,0:T(8,128)(2,1)}, u32[]{:S(2)}) copy-start(bf16[144,160]{1,0:T(8,128)(2,1)} %constant.19.clone.order_ref) | copy-start | bytes 138244
  40.1 4.9 %collective-permute-start.2 = (bf16[216,512]{1,0:T(8,128)(2,1)S(1)}, bf16[216,512]{1,0:T(8,128)(2,1)S(1)}, u32[]{:S(2)}, u32[]{:S(2)}) collective-permute-start(bf16[216,512]{1,0:T(8,128)(2,1)S(1)} %get-tuple-element.21.own_ref), channel_id=1, source_target_pairs={{0,64},{64,0},{1,65},{65,1},{2,66},{66,2},{3,67},{67,3},{4,68},{68... | collective-permute-start | bytes 663560 | tf_op jit(solution)/shard_map/ppermute | solution.py:454
  40.6 9.3 %collective-permute-start.1 = (bf16[216,512]{1,0:T(8,128)(2,1)S(1)}, bf16[216,512]{1,0:T(8,128)(2,1)S(1)}, u32[]{:S(2)}, u32[]{:S(2)}) collective-permute-start(bf16[216,512]{1,0:T(8,128)(2,1)S(1)} %get-tuple-element.20.own_ref), channel_id=1, source_target_pairs={{64,8},{8,64},{65,9},{9,65},{66,10},{10,66},{67,11},{11,67},{68,12... | collective-permute-start | bytes 663560 | tf_op jit(solution)/shard_map/ppermute | solution.py:468
  49.1 5.0 %collective-permute-start.4 = (bf16[144,256]{1,0:T(8,128)(2,1)S(1)}, bf16[144,256]{1,0:T(8,128)(2,1)S(1)}, u32[]{:S(2)}, u32[]{:S(2)}) collective-permute-start(bf16[144,256]{1,0:T(8,128)(2,1)S(1)} %get-tuple-element.26), channel_id=1, source_target_pairs={{0,64},{64,0},{1,65},{65,1},{2,66},{66,2},{3,67},{67,3},{4,68},{68... | collective-permute-start | bytes 221192 | tf_op jit(solution)/shard_map/ppermute | solution.py:454
  54.0 1.3 %collective-permute-start.3 = (bf16[144,256]{1,0:T(8,128)(2,1)S(1)}, bf16[144,256]{1,0:T(8,128)(2,1)S(1)}, u32[]{:S(2)}, u32[]{:S(2)}) collective-permute-start(bf16[144,256]{1,0:T(8,128)(2,1)S(1)} %get-tuple-element.24), channel_id=1, source_target_pairs={{0,64},{64,0},{1,65},{65,1},{2,66},{66,2},{3,67},{67,3},{4,68},{68... | collective-permute-start | bytes 221192 | tf_op jit(solution)/shard_map/ppermute | solution.py:454

commit v3 on v2

--- a/solution.py
+++ b/solution.py
@@ -180,14 +180,7 @@
 
 
 def feed_forward(tokens, w_in, w_out):
-    total = None
-    step = 512
-    for i in range(FF // step):
-        cols = slice(i * step, (i + 1) * step)
-        hidden = gelu(dot(tokens, w_in[:, cols])).astype(BF16)
-        part = dot(hidden, w_out[cols, :])
-        total = part if total is None else total + part
-    return total
+    return dot(gelu(dot(tokens, w_in[...])).astype(BF16), w_out[...])
 
 
 def fetch(sources, targets, sems):
@@ -494,15 +487,17 @@
     )
     got_edge = swap(send_edge)
     first = section == 0
-    out = jnp.concatenate(
+    ready = jnp.concatenate(
         [
-            jnp.where(first, keep_edge, got_edge),
+            keep_edge,
             jnp.where(first, keep_side, got_side),
             jnp.where(first, got_side, keep_side),
-            jnp.where(first, got_edge, keep_edge),
+            keep_edge,
         ],
         axis=0,
     )
+    place = jnp.where(first, 3 * TOKENS, 0)
+    out = lax.dynamic_update_slice(ready, got_edge, (place, 0))
     return out.reshape(1, 8, LATENTS, 24, HALF).transpose(0, 1, 3, 2, 4)
 
 

time: 56.8 us -> 56.3 us (level)
  Pallas kernels: 22.1 us -> 21.1 us
  other arithmetic: 0.77 us -> 0.04 us
  local copies, waits for them, and re-layouts: 0.03 us -> 0.74 us
    pallas_call x2, Pallas kernels: 8.06 us -> 7.32 us  [second_layer(): pl.pallas_call(edge_kernel if at_edge else side_kernel, out_shape=[jax.Sh...]
    concatenate x1, other arithmetic: 0.73 us -> 0.02 us  [on_device(): jnp.concatenate([keep_edge, jnp.where(first, keep_side, got_side), jnp.wh...]
    unnamed x12 -> x14, local copies, waits for them, and re-layouts: 0.03 us -> 0.73 us
  transfers between devices with their start and end apart: 5 -> 5, of which waited for: 3 -> 3; matrix products, arithmetic and copies ran while one was open for 0% -> 0% of each run, Pallas kernels for 14% -> 13%
where the time goes in v3:
time: 56.3 us; the launch traced here: 55.5 us
  blocking collectives  21.4 us (38%)
  Pallas kernels  21.1 us (37%)
  starting transfers between devices  8.03 us (14%)
  waiting for transfers between devices  4.01 us (7%)
  local copies, waits for them, and re-layouts  0.74 us (1%)
    all_to_all x1, blocking collectives, on_device(): lax.all_to_all(pieces.reshape(64, CHUNK, 128), ('lat', 'lon'), split_axis...  21.4 us
    pallas_call x1, Pallas kernels, first_layer(): pl.pallas_call(first_kernel, out_shape=[jax.ShapeDtypeStruct((WIDE, D), B...  7.68 us
    pallas_call x2, Pallas kernels, second_layer(): pl.pallas_call(edge_kernel if at_edge else side_kernel, out_shape=[jax.Sh...  7.32 us
    pallas_call x1, Pallas kernels, encode(): pl.pallas_call(encode_kernel, out_shape=[jax.ShapeDtypeStruct((steps * 16...  6.15 us
    ppermute x1, starting transfers between devices, across(): return lax.ppermute(value, ALL_AXES, pairs)  4.45 us
    ppermute x4, starting transfers between devices, swap(): return lax.ppermute(value, 'section', [(0, 1), (1, 0)])  3.58 us
    ppermute x4, waiting for transfers between devices, swap(): return lax.ppermute(value, 'section', [(0, 1), (1, 0)])  2.92 us
  transfers between devices with their start and end apart: 5, of which 3 were waited for; matrix products, arithmetic and copies ran while one was open for 0% of the time, Pallas kernels for 13%

profile of v3, /device:TPU:7, one launch (start us, length us, event | category | flops | bytes accessed | tf_op | source)
XLA Modules:
  0.0 55.5 jit_solution(18071938781001313972)
XLA Ops:
  0.0 0.0 copy-start.4
  0.0 0.0 copy-start.5
  0.0 6.1 %encode_levels.1 = (bf16[2560,128]{1,0:T(8,128)(2,1)S(1)}, bf16[512,512]{1,0:T(8,128)(2,1)S(1)}, bf16[512,2048]{1,0:T(8,128)(2,1)S(1)}, bf16[2048,512]{1,0:T(8,128)(2,1)S(1)}) custom-call(bf16[2496,512]{1,0:T(8,128)(2,1)} %bitcast.12, bf16[3,512]{1,0:T(4,128)(2,1)} %query_ref.1, bf16[4,512,512]{2,1,0:T(8,128)(2,1)} %w_hbm.1, ...), custom_call_target="tpu_custom_call" | custom-call | tf_op jit(solution)/shard_map/encode_levels/pallas_call | solution.py:277
  6.2 21.4 %all_to_all.5 = bf16[64,40,128]{2,1,0:T(8,128)(2,1)S(1)} all-to-all(bf16[64,40,128]{2,1,0:T(8,128)(2,1)S(1)} %bitcast.11), channel_id=1, replica_groups=mesh['section'=2,'lat'=8,'lon'=8] {'lat','lon'}, dimensions={0} | all-to-all | bytes 1310720 | tf_op jit(solution)/shard_map/all_to_all | solution.py:469
  27.5 2.9 %collective-permute-start = (bf16[64,40,128]{2,1,0:T(8,128)(2,1)S(1)}, bf16[64,40,128]{2,1,0:T(8,128)(2,1)S(1)}, u32[]{:S(2)}, u32[]{:S(2)}) collective-permute-start(bf16[64,40,128]{2,1,0:T(8,128)(2,1)S(1)} %all_to_all.5), channel_id=1, source_target_pairs={{0,64},{64,0},{1,65},{65,1},{2,66},{66,2},{3,67},{67,3},{4,68},{68... | collective-permute-start | bytes 1966088 | tf_op jit(solution)/shard_map/ppermute | solution.py:447
  30.5 1.7 %collective-permute-done = bf16[64,40,128]{2,1,0:T(8,128)(2,1)S(1)} collective-permute-done((bf16[64,40,128]{2,1,0:T(8,128)(2,1)S(1)}, bf16[64,40,128]{2,1,0:T(8,128)(2,1)S(1)}, u32[]{:S(2)}, u32[]{:S(2)}) %collective-permute-start) | collective-permute-done | bytes 655392 | tf_op jit(solution)/shard_map/ppermute | solution.py:447
  32.2 0.0 copy-done
  32.2 0.0 copy-done.1
  32.2 0.0 copy-done.2
  32.2 0.0 copy-start.3
  32.2 7.7 %first_layer.1 = (bf16[216,512]{1,0:T(8,128)(2,1)S(1)}, bf16[216,512]{1,0:T(8,128)(2,1)S(1)}) custom-call(bf16[2560,128]{1,0:T(8,128)(2,1)S(1)} %bitcast.9, bf16[2560,128]{1,0:T(8,128)(2,1)S(1)} %bitcast.10, bf16[3,512]{1,0:T(4,128)(2,1)S(1)} %copy-done.5, f32[2,2,512]{2,1,0:T(2,128)S(1)} %copy-done.4, bf16[2,288,640]{2,1,0:T(8,128)(2,1)S(1)} %copy-done.1, ...), custom_call_target="tpu_custom_call" | custom-call | tf_op jit(solution)/shard_map/first_layer/pallas_call | solution.py:357
  39.9 0.5 collective-permute-start.2
  40.4 4.4 %collective-permute-start.1 = (bf16[216,512]{1,0:T(8,128)(2,1)S(1)}, bf16[216,512]{1,0:T(8,128)(2,1)S(1)}, u32[]{:S(2)}, u32[]{:S(2)}) collective-permute-start(bf16[216,512]{1,0:T(8,128)(2,1)S(1)} %get-tuple-element.20.own_ref), channel_id=1, source_target_pairs={{64,8},{8,64},{65,9},{9,65},{66,10},{10,66},{67,11},{11,67},{68,12... | collective-permute-start | bytes 663560 | tf_op jit(solution)/shard_map/ppermute | solution.py:461
  44.8 0.0 collective-permute-done.2.halo_ref
  44.9 0.0 copy-done.3
  44.9 3.7 %second_layer_side.1 = (bf16[144,256]{1,0:T(8,128)(2,1)S(1)}, bf16[144,256]{1,0:T(8,128)(2,1)S(1)}, bf16[4,512,512]{2,1,0:T(8,128)(2,1)S(1)}) custom-call(bf16[216,512]{1,0:T(8,128)(2,1)S(1)} %collective-permute-done.2.halo_ref, bf16[216,512]{1,0:T(8,128)(2,1)S(1)} %get-tuple-element.21.own_ref, f32[2,2,512]{2,1,0:T(2,128)S(1)} %copy-done.4, ...), custom_call_target="tpu_custom_call" | custom-call | tf_op jit(solution)/shard_map/second_layer_side/pallas_call | solution.py:431
  48.6 0.1 collective-permute-start.3
  48.7 1.1 %collective-permute-done.1.halo_ref = bf16[216,512]{1,0:T(8,128)(2,1)S(1)} collective-permute-done((bf16[216,512]{1,0:T(8,128)(2,1)S(1)}, bf16[216,512]{1,0:T(8,128)(2,1)S(1)}, u32[]{:S(2)}, u32[]{:S(2)}) %collective-permute-start.1) | collective-permute-done | bytes 221216 | tf_op jit(solution)/shard_map/ppermute | solution.py:461
  49.7 3.6 %second_layer_edge.1 = (bf16[144,256]{1,0:T(8,128)(2,1)S(1)}, bf16[144,256]{1,0:T(8,128)(2,1)S(1)}) custom-call(bf16[216,512]{1,0:T(8,128)(2,1)S(1)} %collective-permute-done.1.halo_ref, bf16[216,512]{1,0:T(8,128)(2,1)S(1)} %get-tuple-element.20.own_ref, f32[2,2,512]{2,1,0:T(2,128)S(1)} %copy-done.4, bf16[144,160]{1,0:T(8,128)(2,1)S(1)} %copy-done.3, ...), custom_call_target="tpu_custom_call" | custom-call | tf_op jit(solution)/shard_map/second_layer_edge/pallas_call | solution.py:431
  53.4 0.1 collective-permute-start.4
  53.5 0.0 collective-permute-done.3
  53.6 1.2 %collective-permute-done.4 = bf16[144,256]{1,0:T(8,128)(2,1)S(1)} collective-permute-done((bf16[144,256]{1,0:T(8,128)(2,1)S(1)}, bf16[144,256]{1,0:T(8,128)(2,1)S(1)}, u32[]{:S(2)}, u32[]{:S(2)}) %collective-permute-start.4) | collective-permute-done | bytes 73760 | tf_op jit(solution)/shard_map/ppermute | solution.py:447
  54.8 0.0 copy-start.6
  54.8 0.7 %copy-done.6 = bf16[576,256]{1,0:T(8,128)(2,1)} copy-done((bf16[576,256]{1,0:T(8,128)(2,1)}, bf16[576,256]{1,0:T(8,128)(2,1)S(1)}, u32[]{:S(2)}) %copy-start.6) | copy-done | bytes 294936
  (8 shorter events, 0.1 us)
Async XLA Ops:
  0.0 32.2 %copy-start = (bf16[2,4,512,512]{3,2,1,0:T(8,128)(2,1)S(1)}, bf16[2,4,512,512]{3,2,1,0:T(8,128)(2,1)}, u32[]{:S(2)}) copy-start(bf16[2,4,512,512]{3,2,1,0:T(8,128)(2,1)} %proj_ref.3) | copy-start | bytes 12582916
  0.0 32.2 %copy-start.1 = (bf16[2,288,640]{2,1,0:T(8,128)(2,1)S(1)}, bf16[2,288,640]{2,1,0:T(8,128)(2,1)}, u32[]{:S(2)}) copy-start(bf16[2,288,640]{2,1,0:T(8,128)(2,1)} %constant.21.clone.compact_ref) | copy-start | bytes 2211844
  0.0 32.2 %copy-start.2 = (bf16[2,216,432]{2,1,0:T(8,128)(2,1)S(1)}, bf16[2,216,432]{2,1,0:T(8,128)(2,1)}, u32[]{:S(2)}) copy-start(bf16[2,216,432]{2,1,0:T(8,128)(2,1)} %constant.22.clone.bands_ref) | copy-start | bytes 1119748
  0.0 32.2 %copy-start.4 = (f32[2,2,512]{2,1,0:T(2,128)S(1)}, f32[2,2,512]{2,1,0:T(2,128)}, u32[]{:S(2)}) copy-start(f32[2,2,512]{2,1,0:T(2,128)} %gain_ref.5) | copy-start | bytes 24580
  0.0 32.2 %copy-start.5 = (bf16[3,512]{1,0:T(4,128)(2,1)S(1)}, bf16[3,512]{1,0:T(4,128)(2,1)}, u32[]{:S(2)}) copy-start(bf16[3,512]{1,0:T(4,128)(2,1)} %query_ref.1) | copy-start | bytes 9220
  27.5 4.7 %collective-permute-start = (bf16[64,40,128]{2,1,0:T(8,128)(2,1)S(1)}, bf16[64,40,128]{2,1,0:T(8,128)(2,1)S(1)}, u32[]{:S(2)}, u32[]{:S(2)}) collective-permute-start(bf16[64,40,128]{2,1,0:T(8,128)(2,1)S(1)} %all_to_all.5), channel_id=1, source_target_pairs={{0,64},{64,0},{1,65},{65,1},{2,66},{66,2},{3,67},{67,3},{4,68},{68... | collective-permute-start | bytes 1966088 | tf_op jit(solution)/shard_map/ppermute | solution.py:447
  32.2 12.6 %copy-start.3 = (bf16[144,160]{1,0:T(8,128)(2,1)S(1)}, bf16[144,160]{1,0:T(8,128)(2,1)}, u32[]{:S(2)}) copy-start(bf16[144,160]{1,0:T(8,128)(2,1)} %constant.23.clone.order_ref) | copy-start | bytes 138244
  39.9 4.9 %collective-permute-start.2 = (bf16[216,512]{1,0:T(8,128)(2,1)S(1)}, bf16[216,512]{1,0:T(8,128)(2,1)S(1)}, u32[]{:S(2)}, u32[]{:S(2)}) collective-permute-start(bf16[216,512]{1,0:T(8,128)(2,1)S(1)} %get-tuple-element.21.own_ref), channel_id=1, source_target_pairs={{0,64},{64,0},{1,65},{65,1},{2,66},{66,2},{3,67},{67,3},{4,68},{68... | collective-permute-start | bytes 663560 | tf_op jit(solution)/shard_map/ppermute | solution.py:447
  40.4 9.3 %collective-permute-start.1 = (bf16[216,512]{1,0:T(8,128)(2,1)S(1)}, bf16[216,512]{1,0:T(8,128)(2,1)S(1)}, u32[]{:S(2)}, u32[]{:S(2)}) collective-permute-start(bf16[216,512]{1,0:T(8,128)(2,1)S(1)} %get-tuple-element.20.own_ref), channel_id=1, source_target_pairs={{64,8},{8,64},{65,9},{9,65},{66,10},{10,66},{67,11},{11,67},{68,12... | collective-permute-start | bytes 663560 | tf_op jit(solution)/shard_map/ppermute | solution.py:461
  48.6 4.9 %collective-permute-start.3 = (bf16[144,256]{1,0:T(8,128)(2,1)S(1)}, bf16[144,256]{1,0:T(8,128)(2,1)S(1)}, u32[]{:S(2)}, u32[]{:S(2)}) collective-permute-start(bf16[144,256]{1,0:T(8,128)(2,1)S(1)} %get-tuple-element.25), channel_id=1, source_target_pairs={{0,64},{64,0},{1,65},{65,1},{2,66},{66,2},{3,67},{67,3},{4,68},{68... | collective-permute-start | bytes 221192 | tf_op jit(solution)/shard_map/ppermute | solution.py:447
  53.4 1.3 %collective-permute-start.4 = (bf16[144,256]{1,0:T(8,128)(2,1)S(1)}, bf16[144,256]{1,0:T(8,128)(2,1)S(1)}, u32[]{:S(2)}, u32[]{:S(2)}) collective-permute-start(bf16[144,256]{1,0:T(8,128)(2,1)S(1)} %get-tuple-element.26), channel_id=1, source_target_pairs={{0,64},{64,0},{1,65},{65,1},{2,66},{66,2},{3,67},{67,3},{4,68},{68... | collective-permute-start | bytes 221192 | tf_op jit(solution)/shard_map/ppermute | solution.py:447
  54.8 0.7 %copy-start.6 = (bf16[576,256]{1,0:T(8,128)(2,1)}, bf16[576,256]{1,0:T(8,128)(2,1)S(1)}, u32[]{:S(2)}) copy-start(bf16[576,256]{1,0:T(8,128)(2,1)S(1)} %constant_dynamic-update-slice_fusion) | copy-start | bytes 884740

commit v4 on v3

--- a/solution.py
+++ b/solution.py
@@ -227,13 +227,11 @@
     expand = [
         jnp.where(row == l * GROUP + lane, 1.0, 0.0).astype(BF16) for l in range(LATENTS)
     ]
-    for copy in copies[3:5]:
+    for copy in copies[3:]:
         copy.wait()
+    for copy in later:
+        copy.start()
     for step in range(steps):
-        copies[5 + step].wait()
-        if step == 1:
-            for copy in later:
-                copy.start()
         block = x[step]
         value = dot(block, w[2])
         scores = dot(block, keys).reshape(count * 3, LEVELS, 8, 128)
@@ -272,12 +270,12 @@
 def encode(level_tokens, enc_query, enc_weights, expand, contract):
     source = level_tokens.transpose(0, 1, 2, 4, 5, 3, 6).reshape(-1, D)
     scatter = scatter_table()
-    block = 2 * 24 * LEVELS
+    block = 8 * 24 * LEVELS
     steps = source.shape[0] // block
     return pl.pallas_call(
         encode_kernel,
         out_shape=[
-            jax.ShapeDtypeStruct((steps * 16 * CHUNK, 128), BF16),
+            jax.ShapeDtypeStruct((steps * 64 * CHUNK, 128), BF16),
             pltpu.VMEM((D, D), BF16),
             pltpu.VMEM((D, FF), BF16),
             pltpu.VMEM((FF, D), BF16),

time: 56.3 us -> 55.3 us (0.982)
  Pallas kernels: 21.1 us -> 20.2 us
    pallas_call x1, Pallas kernels: 6.15 us -> 5.18 us  [encode(): pl.pallas_call(encode_kernel, out_shape=[jax.ShapeDtypeStruct((steps * 64...]
where the time goes in v4:
time: 55.3 us; the launch traced here: 54.5 us
  blocking collectives  21.4 us (39%)
  Pallas kernels  20.2 us (37%)
  starting transfers between devices  8.01 us (14%)
  waiting for transfers between devices  4 us (7%)
  local copies, waits for them, and re-layouts  0.74 us (1%)
    all_to_all x1, blocking collectives, on_device(): lax.all_to_all(pieces.reshape(64, CHUNK, 128), ('lat', 'lon'), split_axis...  21.4 us
    pallas_call x1, Pallas kernels, first_layer(): pl.pallas_call(first_kernel, out_shape=[jax.ShapeDtypeStruct((WIDE, D), B...  7.68 us
    pallas_call x2, Pallas kernels, second_layer(): pl.pallas_call(edge_kernel if at_edge else side_kernel, out_shape=[jax.Sh...  7.32 us
    pallas_call x1, Pallas kernels, encode(): pl.pallas_call(encode_kernel, out_shape=[jax.ShapeDtypeStruct((steps * 64...  5.18 us
    ppermute x1, starting transfers between devices, across(): return lax.ppermute(value, ALL_AXES, pairs)  4.45 us
    ppermute x4, starting transfers between devices, swap(): return lax.ppermute(value, 'section', [(0, 1), (1, 0)])  3.56 us
    ppermute x4, waiting for transfers between devices, swap(): return lax.ppermute(value, 'section', [(0, 1), (1, 0)])  2.92 us
  transfers between devices with their start and end apart: 5, of which 3 were waited for; matrix products, arithmetic and copies ran while one was open for 0% of the time, Pallas kernels for 13%

profile of v4, /device:TPU:7, one launch (start us, length us, event | category | flops | bytes accessed | tf_op | source)
XLA Modules:
  0.0 54.5 jit_solution(18152782756963816686)
XLA Ops:
  0.0 0.0 copy-start.4
  0.0 0.0 copy-start.5
  0.0 5.2 %encode_levels.1 = (bf16[2560,128]{1,0:T(8,128)(2,1)S(1)}, bf16[512,512]{1,0:T(8,128)(2,1)S(1)}, bf16[512,2048]{1,0:T(8,128)(2,1)S(1)}, bf16[2048,512]{1,0:T(8,128)(2,1)S(1)}) custom-call(bf16[2496,512]{1,0:T(8,128)(2,1)} %bitcast.12, bf16[3,512]{1,0:T(4,128)(2,1)} %query_ref.1, bf16[4,512,512]{2,1,0:T(8,128)(2,1)} %w_hbm.1, ...), custom_call_target="tpu_custom_call" | custom-call | tf_op jit(solution)/shard_map/encode_levels/pallas_call | solution.py:275
  5.2 21.4 %all_to_all.5 = bf16[64,40,128]{2,1,0:T(8,128)(2,1)S(1)} all-to-all(bf16[64,40,128]{2,1,0:T(8,128)(2,1)S(1)} %bitcast.11), channel_id=1, replica_groups=mesh['section'=2,'lat'=8,'lon'=8] {'lat','lon'}, dimensions={0} | all-to-all | bytes 1310720 | tf_op jit(solution)/shard_map/all_to_all | solution.py:467
  26.6 2.9 %collective-permute-start = (bf16[64,40,128]{2,1,0:T(8,128)(2,1)S(1)}, bf16[64,40,128]{2,1,0:T(8,128)(2,1)S(1)}, u32[]{:S(2)}, u32[]{:S(2)}) collective-permute-start(bf16[64,40,128]{2,1,0:T(8,128)(2,1)S(1)} %all_to_all.5), channel_id=1, source_target_pairs={{0,64},{64,0},{1,65},{65,1},{2,66},{66,2},{3,67},{67,3},{4,68},{68... | collective-permute-start | bytes 1966088 | tf_op jit(solution)/shard_map/ppermute | solution.py:445
  29.5 1.7 %collective-permute-done = bf16[64,40,128]{2,1,0:T(8,128)(2,1)S(1)} collective-permute-done((bf16[64,40,128]{2,1,0:T(8,128)(2,1)S(1)}, bf16[64,40,128]{2,1,0:T(8,128)(2,1)S(1)}, u32[]{:S(2)}, u32[]{:S(2)}) %collective-permute-start) | collective-permute-done | bytes 655392 | tf_op jit(solution)/shard_map/ppermute | solution.py:445
  31.2 0.0 copy-done
  31.2 0.0 copy-done.1
  31.2 0.0 copy-done.2
  31.3 0.0 copy-done.5
  31.3 0.0 copy-start.3
  31.3 7.7 %first_layer.1 = (bf16[216,512]{1,0:T(8,128)(2,1)S(1)}, bf16[216,512]{1,0:T(8,128)(2,1)S(1)}) custom-call(bf16[2560,128]{1,0:T(8,128)(2,1)S(1)} %bitcast.9, bf16[2560,128]{1,0:T(8,128)(2,1)S(1)} %bitcast.10, bf16[3,512]{1,0:T(4,128)(2,1)S(1)} %copy-done.5, f32[2,2,512]{2,1,0:T(2,128)S(1)} %copy-done.4, bf16[2,288,640]{2,1,0:T(8,128)(2,1)S(1)} %copy-done.1, ...), custom_call_target="tpu_custom_call" | custom-call | tf_op jit(solution)/shard_map/first_layer/pallas_call | solution.py:355
  39.0 0.5 collective-permute-start.2
  39.4 4.4 %collective-permute-start.1 = (bf16[216,512]{1,0:T(8,128)(2,1)S(1)}, bf16[216,512]{1,0:T(8,128)(2,1)S(1)}, u32[]{:S(2)}, u32[]{:S(2)}) collective-permute-start(bf16[216,512]{1,0:T(8,128)(2,1)S(1)} %get-tuple-element.20.own_ref), channel_id=1, source_target_pairs={{64,8},{8,64},{65,9},{9,65},{66,10},{10,66},{67,11},{11,67},{68,12... | collective-permute-start | bytes 663560 | tf_op jit(solution)/shard_map/ppermute | solution.py:459
  43.9 0.0 collective-permute-done.2.halo_ref
  43.9 3.7 %second_layer_side.1 = (bf16[144,256]{1,0:T(8,128)(2,1)S(1)}, bf16[144,256]{1,0:T(8,128)(2,1)S(1)}, bf16[4,512,512]{2,1,0:T(8,128)(2,1)S(1)}) custom-call(bf16[216,512]{1,0:T(8,128)(2,1)S(1)} %collective-permute-done.2.halo_ref, bf16[216,512]{1,0:T(8,128)(2,1)S(1)} %get-tuple-element.21.own_ref, f32[2,2,512]{2,1,0:T(2,128)S(1)} %copy-done.4, ...), custom_call_target="tpu_custom_call" | custom-call | tf_op jit(solution)/shard_map/second_layer_side/pallas_call | solution.py:429
  47.6 0.1 collective-permute-start.3
  47.7 1.1 %collective-permute-done.1.halo_ref = bf16[216,512]{1,0:T(8,128)(2,1)S(1)} collective-permute-done((bf16[216,512]{1,0:T(8,128)(2,1)S(1)}, bf16[216,512]{1,0:T(8,128)(2,1)S(1)}, u32[]{:S(2)}, u32[]{:S(2)}) %collective-permute-start.1) | collective-permute-done | bytes 221216 | tf_op jit(solution)/shard_map/ppermute | solution.py:459
  48.8 3.6 %second_layer_edge.1 = (bf16[144,256]{1,0:T(8,128)(2,1)S(1)}, bf16[144,256]{1,0:T(8,128)(2,1)S(1)}) custom-call(bf16[216,512]{1,0:T(8,128)(2,1)S(1)} %collective-permute-done.1.halo_ref, bf16[216,512]{1,0:T(8,128)(2,1)S(1)} %get-tuple-element.20.own_ref, f32[2,2,512]{2,1,0:T(2,128)S(1)} %copy-done.4, bf16[144,160]{1,0:T(8,128)(2,1)S(1)} %copy-done.3, ...), custom_call_target="tpu_custom_call" | custom-call | tf_op jit(solution)/shard_map/second_layer_edge/pallas_call | solution.py:429
  52.4 0.1 collective-permute-start.4
  52.5 0.0 collective-permute-done.3
  52.6 1.2 %collective-permute-done.4 = bf16[144,256]{1,0:T(8,128)(2,1)S(1)} collective-permute-done((bf16[144,256]{1,0:T(8,128)(2,1)S(1)}, bf16[144,256]{1,0:T(8,128)(2,1)S(1)}, u32[]{:S(2)}, u32[]{:S(2)}) %collective-permute-start.4) | collective-permute-done | bytes 73760 | tf_op jit(solution)/shard_map/ppermute | solution.py:445
  53.8 0.0 copy-start.6
  53.8 0.7 %copy-done.6 = bf16[576,256]{1,0:T(8,128)(2,1)} copy-done((bf16[576,256]{1,0:T(8,128)(2,1)}, bf16[576,256]{1,0:T(8,128)(2,1)S(1)}, u32[]{:S(2)}) %copy-start.6) | copy-done | bytes 294936
  (8 shorter events, 0.1 us)
Async XLA Ops:
  0.0 31.2 %copy-start = (bf16[2,4,512,512]{3,2,1,0:T(8,128)(2,1)S(1)}, bf16[2,4,512,512]{3,2,1,0:T(8,128)(2,1)}, u32[]{:S(2)}) copy-start(bf16[2,4,512,512]{3,2,1,0:T(8,128)(2,1)} %proj_ref.3) | copy-start | bytes 12582916
  0.0 31.2 %copy-start.1 = (bf16[2,288,640]{2,1,0:T(8,128)(2,1)S(1)}, bf16[2,288,640]{2,1,0:T(8,128)(2,1)}, u32[]{:S(2)}) copy-start(bf16[2,288,640]{2,1,0:T(8,128)(2,1)} %constant.21.clone.compact_ref) | copy-start | bytes 2211844
  0.0 31.2 %copy-start.2 = (bf16[2,216,432]{2,1,0:T(8,128)(2,1)S(1)}, bf16[2,216,432]{2,1,0:T(8,128)(2,1)}, u32[]{:S(2)}) copy-start(bf16[2,216,432]{2,1,0:T(8,128)(2,1)} %constant.22.clone.bands_ref) | copy-start | bytes 1119748
  0.0 31.2 %copy-start.4 = (f32[2,2,512]{2,1,0:T(2,128)S(1)}, f32[2,2,512]{2,1,0:T(2,128)}, u32[]{:S(2)}) copy-start(f32[2,2,512]{2,1,0:T(2,128)} %gain_ref.5) | copy-start | bytes 24580
  0.0 31.2 %copy-start.5 = (bf16[3,512]{1,0:T(4,128)(2,1)S(1)}, bf16[3,512]{1,0:T(4,128)(2,1)}, u32[]{:S(2)}) copy-start(bf16[3,512]{1,0:T(4,128)(2,1)} %query_ref.1) | copy-start | bytes 9220
  26.6 4.7 %collective-permute-start = (bf16[64,40,128]{2,1,0:T(8,128)(2,1)S(1)}, bf16[64,40,128]{2,1,0:T(8,128)(2,1)S(1)}, u32[]{:S(2)}, u32[]{:S(2)}) collective-permute-start(bf16[64,40,128]{2,1,0:T(8,128)(2,1)S(1)} %all_to_all.5), channel_id=1, source_target_pairs={{0,64},{64,0},{1,65},{65,1},{2,66},{66,2},{3,67},{67,3},{4,68},{68... | collective-permute-start | bytes 1966088 | tf_op jit(solution)/shard_map/ppermute | solution.py:445
  31.3 12.6 %copy-start.3 = (bf16[144,160]{1,0:T(8,128)(2,1)S(1)}, bf16[144,160]{1,0:T(8,128)(2,1)}, u32[]{:S(2)}) copy-start(bf16[144,160]{1,0:T(8,128)(2,1)} %constant.23.clone.order_ref) | copy-start | bytes 138244
  39.0 4.9 %collective-permute-start.2 = (bf16[216,512]{1,0:T(8,128)(2,1)S(1)}, bf16[216,512]{1,0:T(8,128)(2,1)S(1)}, u32[]{:S(2)}, u32[]{:S(2)}) collective-permute-start(bf16[216,512]{1,0:T(8,128)(2,1)S(1)} %get-tuple-element.21.own_ref), channel_id=1, source_target_pairs={{0,64},{64,0},{1,65},{65,1},{2,66},{66,2},{3,67},{67,3},{4,68},{68... | collective-permute-start | bytes 663560 | tf_op jit(solution)/shard_map/ppermute | solution.py:445
  39.4 9.3 %collective-permute-start.1 = (bf16[216,512]{1,0:T(8,128)(2,1)S(1)}, bf16[216,512]{1,0:T(8,128)(2,1)S(1)}, u32[]{:S(2)}, u32[]{:S(2)}) collective-permute-start(bf16[216,512]{1,0:T(8,128)(2,1)S(1)} %get-tuple-element.20.own_ref), channel_id=1, source_target_pairs={{64,8},{8,64},{65,9},{9,65},{66,10},{10,66},{67,11},{11,67},{68,12... | collective-permute-start | bytes 663560 | tf_op jit(solution)/shard_map/ppermute | solution.py:459
  47.6 4.9 %collective-permute-start.3 = (bf16[144,256]{1,0:T(8,128)(2,1)S(1)}, bf16[144,256]{1,0:T(8,128)(2,1)S(1)}, u32[]{:S(2)}, u32[]{:S(2)}) collective-permute-start(bf16[144,256]{1,0:T(8,128)(2,1)S(1)} %get-tuple-element.25), channel_id=1, source_target_pairs={{0,64},{64,0},{1,65},{65,1},{2,66},{66,2},{3,67},{67,3},{4,68},{68... | collective-permute-start | bytes 221192 | tf_op jit(solution)/shard_map/ppermute | solution.py:445
  52.4 1.3 %collective-permute-start.4 = (bf16[144,256]{1,0:T(8,128)(2,1)S(1)}, bf16[144,256]{1,0:T(8,128)(2,1)S(1)}, u32[]{:S(2)}, u32[]{:S(2)}) collective-permute-start(bf16[144,256]{1,0:T(8,128)(2,1)S(1)} %get-tuple-element.26), channel_id=1, source_target_pairs={{0,64},{64,0},{1,65},{65,1},{2,66},{66,2},{3,67},{67,3},{4,68},{68... | collective-permute-start | bytes 221192 | tf_op jit(solution)/shard_map/ppermute | solution.py:445
  53.8 0.7 %copy-start.6 = (bf16[576,256]{1,0:T(8,128)(2,1)}, bf16[576,256]{1,0:T(8,128)(2,1)S(1)}, u32[]{:S(2)}) copy-start(bf16[576,256]{1,0:T(8,128)(2,1)S(1)} %constant_dynamic-update-slice_fusion) | copy-start | bytes 884740
